TPU v7x, 512 devices: a whole 4x4x16 slice. The times are simulated.
512 devices in a mesh: rows: 128 (over z_hi, x, y, core), cols: 4 (over z_lo).
Axes of the slice: x: 4, y: 4, z: 16 (z_hi: 4, z_lo: 4; z = z_hi * 4 + z_lo), core: 2. Of those that a mesh axis runs over, the one named last changes fastest.
Arguments:
- features: bfloat16 [8192, 512], P('rows', 'cols'), may hold values from -6 to 6
- weight: bfloat16 [512, 512], replicated, may hold values from -0.25 to 0.25
- cotangent: bfloat16 [32768, 512], P(('rows', 'cols')), may hold values from -6 to 6
- tile_slot: int32 [128, 32], P('rows'), may hold values from 0 to 127, as said below
- tile_count: int32 [128], P('rows'), may hold values from 8 to 32, as said below
- tile_edges: int32 [128, 32, 512], P('rows'), may hold values from 0 to 16383
- deg_dst: int32 [32768], P('rows'), may hold values from 0 to 1023
- deg_src: int32 [8192], P('rows'), may hold values from 0 to 1023
Outputs:
- activated: bfloat16 [32768, 512], P(('rows', 'cols'))
- weight_grad: float32 [512, 512], replicated
- feature_grad: bfloat16 [8192, 512], P('rows', 'cols')
Inputs may be any that keep to these rules, and one draw needn't show every extreme that they name: `tile_slot`: within one row block the 32 slot numbers are distinct. Only the first tile_count[b] slots of row block b are in use; tile_slot and tile_edges of later slots are ignored.
All inputs are finite; a program needn't handle non-finite values.
Results may differ from a plain program's by a relative error of at most 0.0059.
Values may be sent and summed in bfloat16 or wider, within the bound.
No kernel may reach another device: no remote copies, remote signals or barrier semaphores. Data moves between devices by JAX's collectives and lax.ppermute only.
A program may use at most 64 MiB of HBM per device.

v0:
```python
import math

import jax
import jax.numpy as jnp
from jax import lax
from jax.sharding import PartitionSpec as P

TILE = 128
NB = 256


SQRT_TWO_PI = 0.7978845608028654
CUBIC = 0.044715


def gelu_parts(values):
    inner = SQRT_TWO_PI * (values + CUBIC * values * values * values)
    tanh_val = jnp.tanh(inner)
    output = 0.5 * values * (1.0 + tanh_val)
    slope = 0.5 * (1.0 + tanh_val) + 0.5 * values * (1.0 - tanh_val * tanh_val) * SQRT_TWO_PI * (
        1.0 + 3.0 * CUBIC * values * values
    )
    return (output, slope)


def expand_tiles(edge_ids, live_mask):
    count_all = edge_ids.shape[0]
    group_size = math.gcd(count_all, 8)
    positions = jnp.arange(TILE, dtype=jnp.int32)

    def build(entries):
        group_edges, group_live = entries
        onehot_row = (group_edges[..., None] // TILE == positions).astype(jnp.bfloat16)
        onehot_col = (group_edges[..., None] % TILE == positions).astype(jnp.bfloat16)
        counts = jnp.einsum(
            "ger,gec->grc", onehot_row, onehot_col, preferred_element_type=jnp.float32
        )
        return (counts * group_live[:, None, None]).astype(jnp.bfloat16)

    grouped_edges = edge_ids.reshape(count_all // group_size, group_size, edge_ids.shape[1])
    grouped_live = live_mask.reshape(count_all // group_size, group_size)
    built = lax.map(build, (grouped_edges, grouped_live))
    return built.reshape(count_all, TILE, TILE)


def local(features, weight, cotangent, tile_slot, tile_count, tile_edges, deg_dst, deg_src):
    col_count = lax.axis_size("cols")
    col_index = lax.axis_index("cols")
    panel_width = features.shape[1]
    source_rows = features.shape[0] * lax.axis_size("rows")
    col_tiles = source_rows // TILE
    row_tiles = NB // TILE
    slots = tile_slot[0]
    edge_ids = tile_edges[0]
    slot_total = slots.shape[0]
    live_mask = (jnp.arange(slot_total) < tile_count[0]).astype(jnp.float32)
    src_scale = lax.rsqrt(1.0 + deg_src.astype(jnp.float32))
    dst_scale = lax.rsqrt(1.0 + deg_dst.astype(jnp.float32))
    scaled = (features.astype(jnp.float32) * src_scale[:, None]).astype(jnp.bfloat16)
    gathered_sources = lax.all_gather(scaled, "rows", axis=0, tiled=True)
    tiles = expand_tiles(edge_ids, live_mask)
    group_size = math.gcd(slot_total, 8)
    group_total = slot_total // group_size
    grouped = (
        tiles.reshape(group_total, group_size, TILE, TILE),
        (slots // col_tiles).reshape(group_total, group_size),
        (slots % col_tiles).reshape(group_total, group_size),
    )
    source_blocks = gathered_sources.reshape(col_tiles, TILE, panel_width)

    def forward_step(running, entries):
        tile_group, row_group, col_group = entries
        picked = jnp.take(source_blocks, col_group, axis=0)
        product = jnp.einsum("grc,gcf->grf", tile_group, picked, preferred_element_type=jnp.float32)
        return (running.at[row_group].add(product), None)

    forward_init = jnp.zeros((row_tiles, TILE, panel_width), jnp.float32)
    forward_sum, _ = lax.scan(forward_step, forward_init, grouped)
    aggregated = (forward_sum.reshape(NB, panel_width) * dst_scale[:, None]).astype(jnp.bfloat16)
    row_view = lax.all_to_all(aggregated, "cols", split_axis=0, concat_axis=1, tiled=True)
    pre_act = jnp.dot(row_view, weight, preferred_element_type=jnp.float32)
    output, slope = gelu_parts(pre_act)
    activated = output.astype(jnp.bfloat16)
    pre_grad = (cotangent.astype(jnp.float32) * slope).astype(jnp.bfloat16)
    sub_rows = NB // col_count
    own_terms = jnp.einsum("nf,ng->fg", row_view, pre_grad, preferred_element_type=jnp.float32)
    weight_grad = lax.psum(own_terms, ("rows", "cols"))
    local_scale = lax.dynamic_slice_in_dim(dst_scale, col_index * sub_rows, sub_rows, 0)
    spread_rows = jnp.einsum("ng,fg->nf", pre_grad, weight, preferred_element_type=jnp.float32)
    spread_rows = (spread_rows * local_scale[:, None]).astype(jnp.bfloat16)
    spread_panel = lax.all_to_all(spread_rows, "cols", split_axis=1, concat_axis=0, tiled=True)
    grad_blocks = spread_panel.reshape(row_tiles, TILE, panel_width)

    def backward_step(running, entries):
        tile_group, row_group, col_group = entries
        picked = jnp.take(grad_blocks, row_group, axis=0)
        product = jnp.einsum("grc,grf->gcf", tile_group, picked, preferred_element_type=jnp.float32)
        return (running.at[col_group].add(product), None)

    backward_init = jnp.zeros((col_tiles, TILE, panel_width), jnp.float32)
    backward_sum, _ = lax.scan(backward_step, backward_init, grouped)
    source_terms = backward_sum.reshape(source_rows, panel_width)
    owned = lax.psum_scatter(source_terms, "rows", scatter_dimension=0, tiled=True)
    feature_grad = (owned * src_scale[:, None]).astype(jnp.bfloat16)
    return (activated, weight_grad, feature_grad)


def solution(mesh):
    in_specs = (
        P("rows", "cols"),
        P(),
        P(("rows", "cols"), None),
        P("rows", None),
        P("rows"),
        P("rows", None, None),
        P("rows"),
        P("rows"),
    )
    out_specs = (P(("rows", "cols"), None), P(), P("rows", "cols"))
    return jax.shard_map(local, mesh=mesh, in_specs=in_specs, out_specs=out_specs, check_vma=False)
```

profile of v0, /device:TPU:1, one launch (start us, length us, event | category | flops | bytes accessed | tf_op | source)
XLA Modules:
  0.0 1471.3 jit_solution(11014557895033802390)
XLA Ops:
  7.2 0.7 add_rsqrt_fusion.1
  7.9 1.4 multiply_convert_fusion.3
  9.4 0.6 broadcast.302
  9.9 1.4 reduce.3
  12.0 0.7 add_rsqrt_fusion
  12.8 9.2 while.36
  12.8 0.7 add_select_fusion.6
  13.6 0.7 add_select_fusion.7
  14.3 0.8 fusion.77
  15.2 0.7 add_select_fusion.6
  15.9 0.7 add_select_fusion.7
  16.6 0.8 fusion.77
  17.5 0.7 add_select_fusion.6
  18.2 0.7 add_select_fusion.7
  19.0 0.8 fusion.77
  19.8 0.7 add_select_fusion.6
  20.5 0.7 add_select_fusion.7
  21.3 0.8 fusion.77
  22.1 100.7 %all-gather.2.cloned.1.call-done = bf16[8192,128]{1,0:T(8,128)(2,1)} async-done(((bf16[64,128]{1,0:T(8,128)(2,1)}), bf16[8192,128]{1,0:T(8,128)(2,1)}) %all-gather.2.cloned.1.call-update) | async-done | bytes 2097168 | tf_op jit(solution)/shard_map/all_gather | solution.py:60
  122.8 14.4 while.34
  122.8 2.2 gather_fusion
  125.4 1.0 scatter_fusion
  126.4 2.2 gather_fusion
  129.0 1.0 scatter_fusion
  130.0 2.2 gather_fusion
  132.6 1.0 scatter_fusion
  133.6 2.2 gather_fusion
  136.2 1.0 scatter_fusion
  137.2 0.7 multiply_convert_fusion.1
  137.9 3.7 all-to-all-start
  141.7 4.5 all-to-all-done
  146.2 0.9 multiply_convert_fusion
  147.4 7.0 all_to_all.32
  154.4 2.5 broadcast_in_dim.51
  156.8 14.7 %while.35 = (s32[]{:T(128)}, f32[64,128,128]{2,1,0:T(8,128)}, s32[4,8]{1,0:T(4,128)S(1)}, bf16[4,8,128,128]{3,2,1,0:T(8,128)(2,1)S(1)}, s32[4,8]{1,0:T(4,128)S(1)}, /*index=5*/bf16[2,128,128]{2,1,0:T(8,128)(2,1)S(1)}, s32[]{:T(128)}) while((s32[]{:T(128)}, f32[64,128,128]{2,1,0:T(8,128)}, s32[4,8]{1,0:T(4,128)S(1)}, ...), condition=%wide.region_8.9_spmd, body=%wide.region_6.8_spmd.sunk | while | flops 33817696 | bytes 3150689 | solution.py:101
  156.8 0.6 gather_fusion.1
  157.8 2.7 scatter_fusion.1
  160.5 0.6 gather_fusion.1
  161.4 2.8 scatter_fusion.1
  164.2 0.6 gather_fusion.1
  165.1 2.7 scatter_fusion.1
  167.9 0.6 gather_fusion.1
  168.8 2.7 scatter_fusion.1
  171.6 1.3 fusion.44
  173.0 814.9 %reduce-scatter.2.cloned.1.call-done = f32[64,128]{1,0:T(8,128)} async-done(((f32[8192,128]{1,0:T(8,128)}), f32[64,128]{1,0:T(8,128)}) %reduce-scatter.2.cloned.1.call-update) | async-done | bytes 32784 | tf_op jit(solution)/shard_map/reduce_scatter | solution.py:103
  987.9 1.4 multiply_convert_fusion.2
  989.3 473.2 %all-reduce.2.cloned.1.call-done = f32[512,512]{1,0:T(8,128)} async-done(((f32[512,512]{1,0:T(8,128)}), f32[512,512]{1,0:T(8,128)}) %all-reduce.2.cloned.1.call-update) | async-done | bytes 1048592 | tf_op jit(solution)/shard_map/psum | solution.py:87
  1462.5 2.3 copy.68
  (55 shorter events, 3.4 us)
Async XLA Ops:
  7.2 139.1 %copy-start = (bf16[512,512]{1,0:T(8,128)(2,1)S(1)}, bf16[512,512]{1,0:T(8,128)(2,1)}, u32[]{:S(2)}) copy-start(bf16[512,512]{1,0:T(8,128)(2,1)} %param.15) | copy-start | bytes 1572868
  7.2 115.6 %all-gather.2.cloned.1.call-start = ((), (), s32[]{:S(2)}) async-start(), calls=%async_computation.3 | async-start | bytes 2113536 | tf_op jit(solution)/shard_map/all_gather | solution.py:60
  122.8 24.3 %copy-start.1 = (bf16[64,512]{1,0:T(8,128)(2,1)S(1)}, bf16[64,512]{1,0:T(8,128)(2,1)}, u32[]{:S(2)}) copy-start(bf16[64,512]{1,0:T(8,128)(2,1)} %param.16) | copy-start | bytes 196612
  137.9 8.3 all-to-all-start
  141.6 846.2 %reduce-scatter.2.cloned.1.call-start = ((), (), s32[]{:S(2)}) async-start(), calls=%async_computation.5 | async-start | bytes 4227072 | tf_op jit(solution)/shard_map/reduce_scatter | solution.py:103
  171.6 1290.9 %all-reduce.2.cloned.1.call-start = ((), (), s32[]{:S(2)}) async-start(), calls=%async_computation.4 | async-start | bytes 2097152 | tf_op jit(solution)/shard_map/psum | solution.py:87
Sparse Core Ops, SparseCore 0:
  13.0 109.6 all-gather.1
  171.7 816.1 reduce-scatter.1
  994.8 467.6 all-reduce.1
where the time goes:
time: 1470 us
  waiting for transfers between devices  1390 us (95%)
  other arithmetic  27.5 us (2%)
  local copies, waits for them, and re-layouts  16.8 us (1%)
    reduce_scatter x1, waiting for transfers between devices, local(): lax.psum_scatter(source_terms, 'rows', scatter_dimension=0, tiled=True)  815 us
    psum x1, waiting for transfers between devices, local(): weight_grad = lax.psum(own_terms, ('rows', 'cols'))  473 us
    all_gather x1, waiting for transfers between devices, local(): gathered_sources = lax.all_gather(scaled, 'rows', axis=0, tiled=True)  101 us
  transfers between devices with their start and end apart: 4, of which 4 were waited for; matrix products, arithmetic and copies ran while one was open for 1% of the time, Pallas kernels for 0%

commit v1 on v0

v1 whole, which is shorter than its diff:
```python
import jax
import jax.numpy as jnp
from jax import lax
from jax.experimental import pallas as pl
from jax.experimental.pallas import tpu as pltpu
from jax.sharding import Mesh, PartitionSpec as P

TILE = 128
NB = 256
SUB = 64
SLOTS = 32
SQRT_TWO_PI = 0.7978845608028654
CUBIC = 0.044715
ROWS = ("zh", "x", "y", "c")
PLANE = ("x", "y", "c")
RING = ("zh", "zl")
FINE = (("zh", 4), ("x", 4), ("y", 4), ("c", 2), ("zl", 4))

VMEM = pl.BlockSpec(memory_space=pltpu.VMEM)
SMEM = pl.BlockSpec(memory_space=pltpu.SMEM)


def call(kernel, out_shape, in_specs, scratch=(), micros=2, name=None):
    single = not isinstance(out_shape, (tuple, list))
    return pl.pallas_call(
        kernel,
        out_shape=out_shape,
        in_specs=in_specs,
        out_specs=VMEM if single else [VMEM] * len(out_shape),
        scratch_shapes=list(scratch),
        compiler_params=pltpu.CompilerParams(vmem_limit_bytes=24 * 1024 * 1024),
        cost_estimate=pl.CostEstimate(
            flops=int(micros * 1e9), bytes_accessed=int(micros * 1e6), transcendentals=0
        ),
        name=name,
    )


def gelu_parts(values):
    inner = SQRT_TWO_PI * (values + CUBIC * values * values * values)
    tanh_val = jnp.tanh(inner)
    output = 0.5 * values * (1.0 + tanh_val)
    slope = 0.5 * (1.0 + tanh_val) + 0.5 * values * (1.0 - tanh_val * tanh_val) * SQRT_TWO_PI * (
        1.0 + 3.0 * CUBIC * values * values
    )
    return (output, slope)


def column(row):
    n = row.shape[1]
    first = lax.broadcasted_iota(jnp.int32, (n, n), 0)
    second = lax.broadcasted_iota(jnp.int32, (n, n), 1)
    return jnp.sum(jnp.where(first == second, row, 0.0), axis=1, keepdims=True)


def degree_scale(degrees):
    return column(lax.rsqrt(1.0 + degrees.astype(jnp.float32)))


def encode(edges):
    row = edges >> 7
    value = 1.0 + (edges & (TILE - 1)).astype(jnp.float32) * (1.0 / TILE)
    value = value * jnp.float32(2.0**-32)
    for bit in range(6):
        value = value * jnp.where(((row >> bit) & 1) == 1, jnp.float32(2.0 ** (1 << bit)), jnp.float32(1.0))
    return jnp.where(row >= SUB, -value, value)


def decode(values):
    values = values.astype(jnp.float32)
    rest = jnp.abs(values) * jnp.float32(2.0**32)
    row = jnp.where(values < 0.0, SUB, 0)
    for bit in range(5, -1, -1):
        big = rest >= jnp.float32(2.0 ** (1 << bit))
        rest = jnp.where(big, rest * jnp.float32(2.0 ** -(1 << bit)), rest)
        row = row + jnp.where(big, 1 << bit, 0)
    col = ((rest - 1.0) * TILE).astype(jnp.int32)
    return jnp.where(values == 0.0, -1, row * TILE + col)


def onehots(code):
    row = code >> 7
    col = code & (TILE - 1)
    positions = lax.broadcasted_iota(jnp.int32, (TILE, code.shape[1]), 0)
    one = jnp.float32(1.0)
    zero = jnp.float32(0.0)
    return (
        jnp.where(positions == row, one, zero).astype(jnp.bfloat16),
        jnp.where(positions == col, one, zero).astype(jnp.bfloat16),
    )


def nt(left, right):
    return lax.dot_general(left, right, (((1,), (1,)), ((), ())), preferred_element_type=jnp.float32)


def prepare(count_ref, feature_ref, degree_ref, slot_ref, edge_ref, out_ref, scale_ref):
    scale = degree_scale(degree_ref[...])
    scale_ref[...] = scale
    scaled = (feature_ref[...].astype(jnp.float32) * scale).astype(jnp.bfloat16)
    count = count_ref[0]
    live = lax.broadcasted_iota(jnp.int32, edge_ref.shape, 0) < count
    codes = jnp.where(live, encode(edge_ref[...]), 0.0).astype(jnp.bfloat16)
    used = lax.broadcasted_iota(jnp.int32, (1, SLOTS), 1) < count
    slots = jnp.where(used, slot_ref[...], -1).astype(jnp.float32)
    slots = jnp.concatenate([slots, jnp.zeros((1, TILE - SLOTS), jnp.float32)], axis=1)
    slots = jnp.broadcast_to(slots, (16, TILE)).astype(jnp.bfloat16)
    for i in range(4):
        out_ref[i, 0:SUB, :] = scaled
        for p in range(4):
            out_ref[i, SUB + p * SLOTS:SUB + (p + 1) * SLOTS, :] = codes[:, p * TILE:(p + 1) * TILE]
        out_ref[i, 192:208, :] = slots


def build_forward(slot_ref, count_ref, edge_ref, wide_ref):
    wide_ref[...] = jnp.zeros_like(wide_ref)
    count = count_ref[0]

    def step(group, carry):
        for k in range(4):
            j = group * 4 + k
            row, col = onehots(jnp.where(j < count, edge_ref[pl.ds(j, 1), :], -1))
            tile = nt(row, col).astype(jnp.bfloat16)
            row_at = pl.multiple_of((slot_ref[j] >> 6) * TILE, TILE)
            wide_ref[pl.ds(row_at, TILE), pl.ds(pl.multiple_of(j * TILE, TILE), TILE)] = tile
        return carry

    lax.fori_loop(0, (count + 3) >> 2, step, 0)


def build_backward(slot_ref, quarter_ref, ring_ref, out_ref, list_ref, code_ref):
    out_ref[...] = jnp.zeros_like(out_ref)
    for i in range(4):
        code_ref[i * TILE:(i + 1) * TILE, :] = decode(ring_ref[i, SUB:192, :])
    quarter = quarter_ref[0]
    total = slot_ref.shape[0]

    def scan(i, n):
        slot = slot_ref[i]
        hit = jnp.logical_and(slot >= 0, ((slot & 63) >> 4) == quarter)

        @pl.when(hit)
        def _():
            for k in range(4):
                list_ref[n + k] = i

        return n + hit.astype(jnp.int32)

    found = lax.fori_loop(0, total, scan, 0)

    def step(group, carry):
        for k in range(4):
            i = list_ref[group * 4 + k]
            slot = slot_ref[i]
            block = i >> 5
            at = block * TILE + (i & 31)
            code = jnp.concatenate([code_ref[pl.ds(at + p * SLOTS, 1), :] for p in range(4)], axis=1)
            row, col = onehots(code)
            tile = nt(col, row).astype(jnp.bfloat16)
            at = pl.multiple_of((slot & 15) * TILE, TILE)
            lane = pl.multiple_of((block * 2 + (slot >> 6)) * TILE, TILE)
            out_ref[pl.ds(at, TILE), pl.ds(lane, TILE)] = tile
        return carry

    lax.fori_loop(0, (found + 3) >> 2, step, 0)


def aggregate(slot_ref, core_ref, wide_ref, own_ref, other_ref, degree_ref, out_ref, picked):
    core = core_ref[0]
    for j in range(SLOTS):
        tile = slot_ref[j] & 63
        at = pl.multiple_of(((tile & 15) * 4 + (tile >> 4)) * SUB, SUB)
        own_at = pl.multiple_of(j * TILE + core * SUB, SUB)
        other_at = pl.multiple_of(j * TILE + (1 - core) * SUB, SUB)
        picked[pl.ds(own_at, SUB), :] = own_ref[pl.ds(at, SUB), :]
        picked[pl.ds(other_at, SUB), :] = other_ref[pl.ds(at, SUB), :]
    total = jnp.dot(wide_ref[...], picked[...], preferred_element_type=jnp.float32)
    out_ref[...] = (total * degree_scale(degree_ref[...])).astype(jnp.bfloat16)


def dense(part_ref, panel_ref, weight_ref, cot_ref, degree_ref, act_ref, spread_ref, term_ref):
    scale = degree_scale(degree_ref[pl.ds(part_ref[0], 1), :])
    rows = jnp.concatenate([panel_ref[p] for p in range(4)], axis=1)
    pre_act = jnp.dot(rows, weight_ref[...], preferred_element_type=jnp.float32)
    output, slope = gelu_parts(pre_act)
    act_ref[...] = output.astype(jnp.bfloat16)
    pre_grad = (cot_ref[...].astype(jnp.float32) * slope).astype(jnp.bfloat16)
    spread = (nt(pre_grad, weight_ref[...]) * scale).astype(jnp.bfloat16)
    for p in range(4):
        spread_ref[p] = spread[:, p * TILE:(p + 1) * TILE]
    terms = lax.dot_general(rows, pre_grad, (((0,), (0,)), ((), ())), preferred_element_type=jnp.float32)
    term_ref[...] = terms.astype(jnp.bfloat16)


def pack_ring(part_ref, spread_ref, out_ref):
    total = part_ref[0].astype(jnp.float32)
    for s in range(1, part_ref.shape[0]):
        total = total + part_ref[s].astype(jnp.float32)
    total = total.astype(jnp.bfloat16)
    for i in range(16):
        p = i % 4
        out_ref[i, 0:SUB, :] = spread_ref[p]
        out_ref[i, SUB:SUB + 16, :] = total[:, p * TILE:(p + 1) * TILE]


def sum_ring(ring_ref, out_ref):
    total = jnp.zeros((16, TILE), jnp.float32)
    for i in range(16):
        total = total + ring_ref[i, SUB:SUB + 16, :].astype(jnp.float32)
    total = total.astype(jnp.bfloat16)
    for i in range(4):
        out_ref[i] = total


def spread_back(adj_ref, ring_ref, out_ref, grad):
    for i in range(16):
        grad[i * SUB:(i + 1) * SUB, :] = ring_ref[i, 0:SUB, :]
    for block in range(8):
        rows = adj_ref[block * 256:(block + 1) * 256, :]
        terms = jnp.dot(rows, grad[...], preferred_element_type=jnp.float32).astype(jnp.bfloat16)
        for k in range(4):
            out_ref[block * 4 + k] = terms[k * SUB:(k + 1) * SUB, :]


def finish(plane_ref, scale_ref, feature_ref, weight_ref):
    total = plane_ref[0, 0:SUB, :].astype(jnp.float32)
    for s in range(1, 32):
        total = total + plane_ref[s, 0:SUB, :].astype(jnp.float32)
    feature_ref[...] = (total * scale_ref[...]).astype(jnp.bfloat16)
    for s in range(32):
        for p in range(4):
            weight_ref[s * 16:(s + 1) * 16, p * TILE:(p + 1) * TILE] = plane_ref[
                s, SUB + p * 16:SUB + (p + 1) * 16, :
            ].astype(jnp.float32)


def local(features, weight, cotangent, tile_slot, tile_count, tile_edges, deg_dst, deg_src):
    bf16 = jnp.bfloat16
    shape = jax.ShapeDtypeStruct
    zh, core, zl = lax.axis_index("zh"), lax.axis_index("c"), lax.axis_index("zl")
    slots = jnp.clip(tile_slot, 0, 127)
    edges = tile_edges[0]

    piece, src_scale = call(
        prepare,
        (shape((4, 208, TILE), bf16), shape((SUB, 1), jnp.float32)),
        [SMEM, VMEM, VMEM, VMEM, VMEM],
        micros=1,
        name="prepare",
    )(tile_count, features, deg_src[None], slots, edges)
    piece = lax.all_to_all(piece, "zh", 0, 0)
    wide = call(build_forward, shape((NB, SLOTS * TILE), bf16), [SMEM, SMEM, VMEM], micros=6, name="build_forward")(
        slots[0], tile_count, edges
    )
    piece, wide = lax.optimization_barrier((piece, wide))

    plane_sources = lax.all_to_all(jnp.broadcast_to(piece[:, :SUB], (16, 4, SUB, TILE)), ("x", "y"), 0, 0)
    adjacent = call(
        build_backward,
        shape((2048, 1024), bf16),
        [SMEM, SMEM, VMEM],
        [pltpu.SMEM((4 * SLOTS + 8,), jnp.int32), pltpu.VMEM((4 * TILE, TILE), jnp.int32)],
        micros=6,
        name="build_backward",
    )(piece[:, 192, :SLOTS].astype(jnp.int32).reshape(4 * SLOTS), zh[None], piece)
    own_sources = plane_sources.reshape(64 * SUB, TILE)
    own_sources, adjacent = lax.optimization_barrier((own_sources, adjacent))
    other_sources = lax.ppermute(own_sources, "c", [(0, 1), (1, 0)])

    aggregated = call(
        aggregate,
        shape((NB, TILE), bf16),
        [SMEM, SMEM, VMEM, VMEM, VMEM, VMEM],
        [pltpu.VMEM((SLOTS * TILE, TILE), bf16)],
        name="aggregate",
    )(slots[0], core[None], wide, own_sources, other_sources, deg_dst[None])

    panels = lax.all_to_all(aggregated.reshape(4, SUB, TILE), "zl", 0, 0)
    activated, spread, terms = call(
        dense,
        (shape((SUB, 512), bf16), shape((4, SUB, TILE), bf16), shape((512, 512), bf16)),
        [SMEM] + [VMEM] * 4,
        name="dense",
    )(zl[None], panels, weight, cotangent, deg_dst.reshape(4, SUB))

    parts = lax.all_to_all(terms.reshape(32, 16, 512), PLANE, 0, 0)
    ring = call(pack_ring, shape((16, SUB + 16, TILE), bf16), [VMEM] * 2, name="pack_ring")(parts, spread)
    ring = lax.all_to_all(ring, RING, 0, 0)
    panel_sum = call(sum_ring, shape((4, 16, TILE), bf16), [VMEM], micros=1, name="sum_ring")(ring)
    weight_rows = lax.all_to_all(panel_sum, "zl", 0, 0).reshape(SUB, TILE)
    source_terms = call(
        spread_back,
        shape((32, SUB, TILE), bf16),
        [VMEM] * 2,
        [pltpu.VMEM((1024, TILE), bf16)],
        name="spread_back",
    )(adjacent, ring)
    plane = jnp.concatenate([source_terms, jnp.broadcast_to(weight_rows, (32, SUB, TILE))], axis=1)
    plane = lax.all_to_all(plane, PLANE, 0, 0)
    feature_grad, weight_grad = call(
        finish, (shape((SUB, TILE), bf16), shape((512, 512), jnp.float32)), [VMEM] * 2, name="finish"
    )(plane, src_scale)
    return (activated, weight_grad, feature_grad)


def solution(mesh):
    fine = Mesh(mesh.devices.reshape([size for _, size in FINE]), [name for name, _ in FINE])
    in_specs = (
        P(ROWS, "zl"),
        P(),
        P(ROWS + ("zl",), None),
        P(ROWS, None),
        P(ROWS),
        P(ROWS, None, None),
        P(ROWS),
        P(ROWS),
    )
    out_specs = (P(ROWS + ("zl",), None), P(), P(ROWS, "zl"))
    return jax.shard_map(local, mesh=fine, in_specs=in_specs, out_specs=out_specs, check_vma=False)
```

time: 1470 us -> 155 us (0.11)
  waiting for transfers between devices: 1390 us -> 23.4 us
  blocking collectives: 6.96 us -> 61.7 us
  starting transfers between devices: 3.78 us -> 43.1 us
  other arithmetic: 27.5 us -> 0.77 us
    reduce_scatter x1 -> x0, waiting for transfers between devices: 815 us -> none  [local(): lax.psum_scatter(source_terms, 'rows', scatter_dimension=0, tiled=True)]
    psum x1 -> x0, waiting for transfers between devices: 473 us -> none  [local(): weight_grad = lax.psum(own_terms, ('rows', 'cols'))]
    all_gather x1 -> x0, waiting for transfers between devices: 101 us -> none  [local(): gathered_sources = lax.all_gather(scaled, 'rows', axis=0, tiled=True)]
    all_to_all x1 -> x3, blocking collectives: 6.96 us -> 61.7 us  [the longest x1 23.4 us: local(): plane = lax.all_to_all(plane, PLANE, 0, 0)]
    all_to_all x1 -> x4, starting transfers between devices: 3.7 us -> 34.7 us  [the longest x1 15.6 us: local(): piece = lax.all_to_all(piece, 'zh', 0, 0)]
    all_to_all x1 -> x4, waiting for transfers between devices: 4.52 us -> 21.1 us  [the longest x1 9.96 us: local(): piece = lax.all_to_all(piece, 'zh', 0, 0)]
    scatter-add x8 -> x0, other arithmetic: 15 us -> none  [the longest x4 10.9 us: backward_step(): return (running.at[col_group].add(product), None)]
  transfers between devices with their start and end apart: 4 -> 5, of which waited for: 4 -> 5; matrix products, arithmetic and copies ran while one was open for 1% -> 0% of each run, Pallas kernels for 0% -> 5%
where the time goes in v1:
time: 155 us; the launch traced here: 154 us
  blocking collectives  61.7 us (40%)
  starting transfers between devices  43.1 us (28%)
  waiting for transfers between devices  23.4 us (15%)
  Pallas kernels  12.7 us (8%)
  local copies, waits for them, and re-layouts  10.8 us (7%)
    all_to_all x1, blocking collectives, local(): plane = lax.all_to_all(plane, PLANE, 0, 0)  23.4 us
    all_to_all x1, blocking collectives, local(): ring = lax.all_to_all(ring, RING, 0, 0)  21.7 us
    all_to_all x1, blocking collectives, local(): parts = lax.all_to_all(terms.reshape(32, 16, 512), PLANE, 0, 0)  16.7 us
    all_to_all x1, starting transfers between devices, local(): piece = lax.all_to_all(piece, 'zh', 0, 0)  15.6 us
    all_to_all x1, waiting for transfers between devices, local(): piece = lax.all_to_all(piece, 'zh', 0, 0)  9.96 us
    unnamed x22, local copies, waits for them, and re-layouts  9.28 us
    ppermute x1, starting transfers between devices, local(): other_sources = lax.ppermute(own_sources, 'c', [(0, 1), (1, 0)])  8.44 us
    all_to_all x1, starting transfers between devices, local(): lax.all_to_all(jnp.broadcast_to(piece[:, :SUB], (16, 4, SUB, TILE)), ('x'...  6.75 us
  transfers between devices with their start and end apart: 5, of which 5 were waited for; matrix products, arithmetic and copies ran while one was open for 0% of the time, Pallas kernels for 5%

profile of v1, /device:TPU:1, one launch (start us, length us, event | category | flops | bytes accessed | tf_op | source)
XLA Modules:
  0.0 153.8 jit_solution(2514014268544410587)
XLA Ops:
  0.6 0.7 broadcast_clamp_fusion
  1.9 0.0 copy-start.2
  2.0 0.8 copy-done.2
  2.8 0.0 copy-start.5
  2.8 0.7 copy-done.5
  3.5 0.0 copy-start.6
  3.5 0.7 copy-done.6
  4.2 0.0 copy-start.3
  4.2 0.9 prepare.1
  5.0 15.6 %all-to-all-start = ((bf16[4,208,128]{2,1,0:T(8,128)(2,1)}), bf16[4,208,128]{2,1,0:T(8,128)(2,1)S(1)}, u32[]{:S(2)}, u32[]{:S(2)}) async-start(bf16[4,208,128]{2,1,0:T(8,128)(2,1)} %get-tuple-element.14), calls=%async_computation | async-start | bytes 425984 | tf_op jit(solution)/shard_map/all_to_all | solution.py:251
  20.6 0.0 copy-done.3
  20.6 1.7 %build_forward.1.wide_ref = bf16[256,4096]{1,0:T(8,128)(2,1)S(1)} custom-call(s32[32]{0:T(128)S(1)} %get-tuple-element.26.slot_ref, s32[1]{0:T(128)S(6)} %copy.11.count_ref, s32[32,512]{1,0:T(8,128)S(1)} %bitcast.17), custom_call_target="tpu_custom_call" | custom-call | flops 6000000000 | bytes 6000000 | tf_op jit(solution)/shard_map/build_forward/pallas_call | solution.py:252
  22.3 0.0 copy-start.9
  22.3 1.3 copy-done.9
  23.7 10.0 %all-to-all-done.ring_ref = bf16[4,208,128]{2,1,0:T(8,128)(2,1)S(1)} async-done(((bf16[4,208,128]{2,1,0:T(8,128)(2,1)}), bf16[4,208,128]{2,1,0:T(8,128)(2,1)S(1)}, u32[]{:S(2)}, u32[]{:S(2)}) %all-to-all-start) | async-done | bytes 213024 | tf_op jit(solution)/shard_map/all_to_all | solution.py:251
  33.6 1.2 broadcast_in_dim.24
  34.9 6.8 %all-to-all-start.1 = ((bf16[16,4,64,128]{3,2,1,0:T(8,128)(2,1)}), bf16[16,4,64,128]{3,2,1,0:T(8,128)(2,1)S(1)}, u32[]{:S(2)}, u32[]{:S(2)}) async-start(bf16[16,4,64,128]{3,2,1,0:T(8,128)(2,1)} %broadcast_in_dim.24), calls=%async_computation.1 | async-start | bytes 2097152 | tf_op jit(solution)/shard_map/all_to_all | solution.py:257
  41.6 0.1 reshape.30.slot_ref
  41.7 4.1 %build_backward.1.adj_ref = bf16[2048,1024]{1,0:T(8,128)(2,1)S(1)} custom-call(s32[128]{0:T(128)S(1)} %reshape.30.slot_ref, s32[1]{0:T(128)} %bitcast.6.quarter_ref, bf16[4,208,128]{2,1,0:T(8,128)(2,1)S(1)} %all-to-all-done.ring_ref), custom_call_target="tpu_custom_call" | custom-call | flops 6000000000 | bytes 6000000 | tf_op jit(solution)/shard_map/build_backward/pallas_call | solution.py:258
  45.9 0.0 copy-start.7
  45.9 1.9 %copy-done.7 = bf16[2048,1024]{1,0:T(8,128)(2,1)} copy-done((bf16[2048,1024]{1,0:T(8,128)(2,1)}, bf16[2048,1024]{1,0:T(8,128)(2,1)S(1)}, u32[]{:S(2)}) %copy-start.7) | copy-done | bytes 4194328
  47.8 5.7 %all-to-all-done.1 = bf16[16,4,64,128]{3,2,1,0:T(8,128)(2,1)S(1)} async-done(((bf16[16,4,64,128]{3,2,1,0:T(8,128)(2,1)}), bf16[16,4,64,128]{3,2,1,0:T(8,128)(2,1)S(1)}, u32[]{:S(2)}, u32[]{:S(2)}) %all-to-all-start.1) | async-done | bytes 1048608 | tf_op jit(solution)/shard_map/all_to_all | solution.py:257
  53.5 8.4 %collective-permute-start = (bf16[4096,128]{1,0:T(8,128)(2,1)S(1)}, bf16[4096,128]{1,0:T(8,128)(2,1)S(1)}, u32[]{:S(2)}, u32[]{:S(2)}) collective-permute-start(bf16[4096,128]{1,0:T(8,128)(2,1)S(1)} %bitcast.12), channel_id=1, source_target_pairs={{0,4},{4,0},{1,5},{5,1},{2,6},{6,2},{3,7},{7,3},{8,12},{12,8},{9,1... | collective-permute-start | bytes 3145736 | tf_op jit(solution)/shard_map/ppermute | solution.py:268
  61.9 2.3 %collective-permute-done.other_ref = bf16[4096,128]{1,0:T(8,128)(2,1)S(1)} collective-permute-done((bf16[4096,128]{1,0:T(8,128)(2,1)S(1)}, bf16[4096,128]{1,0:T(8,128)(2,1)S(1)}, u32[]{:S(2)}, u32[]{:S(2)}) %collective-permute-start) | collective-permute-done | bytes 1048608 | tf_op jit(solution)/shard_map/ppermute | solution.py:268
  64.2 0.0 copy-done
  64.2 0.0 copy-start.10
  64.2 1.6 %copy-done.10 = bf16[256,4096]{1,0:T(8,128)(2,1)S(1)} copy-done((bf16[256,4096]{1,0:T(8,128)(2,1)S(1)}, bf16[256,4096]{1,0:T(8,128)(2,1)}, u32[]{:S(2)}) %copy-start.10) | copy-done | bytes 2097176
  65.8 0.0 copy-start.1
  65.8 0.0 copy-start.4
  65.8 2.0 %aggregate.1 = bf16[256,128]{1,0:T(8,128)(2,1)} custom-call(s32[32]{0:T(128)S(1)} %get-tuple-element.26.slot_ref, s32[1]{0:T(128)} %bitcast.2.core_ref, bf16[256,4096]{1,0:T(8,128)(2,1)S(1)} %copy-done.10, bf16[4096,128]{1,0:T(8,128)(2,1)S(1)} %bitcast.13, bf16[4096,128]{1,0:T(8,128)(2,1)S(1)} %collective-permute-done.other_ref, s32[1,256]{1,0:T(1,128)S(1)} %bitcast.15), custom_call_target="tpu_custom_call" | custom-call | flops 2000000000 | bytes 2000000 | tf_op jit(solution)/shard_map/aggregate/pallas_call | solution.py:270
  67.8 6.6 %all-to-all-start.2 = ((bf16[4,64,128]{2,1,0:T(8,128)(2,1)}), bf16[4,64,128]{2,1,0:T(8,128)(2,1)S(1)}, u32[]{:S(2)}, u32[]{:S(2)}) async-start(bf16[4,64,128]{2,1,0:T(8,128)(2,1)} %bitcast.8), calls=%async_computation.2 | async-start | bytes 131072 | tf_op jit(solution)/shard_map/all_to_all | solution.py:278
  74.4 0.1 reshape.27.degree_ref
  74.5 4.5 %all-to-all-done.2.panel_ref = bf16[4,64,128]{2,1,0:T(8,128)(2,1)S(1)} async-done(((bf16[4,64,128]{2,1,0:T(8,128)(2,1)}), bf16[4,64,128]{2,1,0:T(8,128)(2,1)S(1)}, u32[]{:S(2)}, u32[]{:S(2)}) %all-to-all-start.2) | async-done | bytes 65568 | tf_op jit(solution)/shard_map/all_to_all | solution.py:278
  79.0 0.0 copy-done.1
  79.0 0.0 copy-done.4
  79.0 0.9 dense.1
  80.0 16.7 %all_to_all.35.part_ref = bf16[32,16,512]{2,1,0:T(8,128)(2,1)S(1)} all-to-all(bf16[32,16,512]{2,1,0:T(8,128)(2,1)S(1)} %bitcast.14), channel_id=1, replica_groups=mesh['zh'=4,'x'=4,'y'=4,'c'=2,'zl'=4] {'x','y','c'}, dimensions={0} | all-to-all | bytes 1048576 | tf_op jit(solution)/shard_map/all_to_all | solution.py:286
  96.6 0.1 pack_ring.1
  96.7 21.7 %all_to_all.36.ring_ref = bf16[16,80,128]{2,1,0:T(8,128)(2,1)S(1)} all-to-all(bf16[16,80,128]{2,1,0:T(8,128)(2,1)S(1)} %pack_ring.1), channel_id=1, replica_groups=mesh['zh'=4,'x'=4,'y'=4,'c'=2,'zl'=4] {'zh','zl'}, dimensions={0} | all-to-all | bytes 655360 | tf_op jit(solution)/shard_map/all_to_all | solution.py:288
  118.4 0.6 sum_ring.1
  119.0 5.7 %all-to-all-start.5 = ((bf16[4,16,128]{2,1,0:T(8,128)(2,1)}), bf16[4,16,128]{2,1,0:T(8,128)(2,1)S(1)}, u32[]{:S(2)}, u32[]{:S(2)}) async-start(bf16[4,16,128]{2,1,0:T(8,128)(2,1)} %sum_ring.1), calls=%async_computation.5 | async-start | bytes 32768 | tf_op jit(solution)/shard_map/all_to_all | solution.py:290
  124.7 2.2 %copy-done.8 = bf16[2048,1024]{1,0:T(8,128)(2,1)S(1)} copy-done((bf16[2048,1024]{1,0:T(8,128)(2,1)S(1)}, bf16[2048,1024]{1,0:T(8,128)(2,1)}, u32[]{:S(2)}) %copy-start.8) | copy-done | bytes 4194328
  126.9 1.3 spread_back.1
  128.2 1.0 all-to-all-done.5
  129.2 0.1 broadcast_in_dim.27
  129.3 0.1 pad_maximum_fusion
  129.4 23.4 %all_to_all.37.plane_ref = bf16[32,128,128]{2,1,0:T(8,128)(2,1)S(1)} all-to-all(bf16[32,128,128]{2,1,0:T(8,128)(2,1)S(1)} %pad_maximum_fusion), channel_id=1, replica_groups=mesh['zh'=4,'x'=4,'y'=4,'c'=2,'zl'=4] {'x','y','c'}, dimensions={0} | all-to-all | bytes 2097152 | tf_op jit(solution)/shard_map/all_to_all | solution.py:299
  152.7 1.1 finish.1
  (4 shorter events, 0.0 us)
Async XLA Ops:
  1.9 0.8 copy-start.2
  2.8 0.7 copy-start.5
  3.5 0.7 copy-start.6
  4.2 16.5 %copy-start.3 = (s32[1,32,512]{2,1,0:T(8,128)S(1)}, s32[1,32,512]{2,1,0:T(8,128)}, u32[]{:S(2)}) copy-start(s32[1,32,512]{2,1,0:T(8,128)} %param.13) | copy-start | bytes 196612
  5.0 28.6 %all-to-all-start = ((bf16[4,208,128]{2,1,0:T(8,128)(2,1)}), bf16[4,208,128]{2,1,0:T(8,128)(2,1)S(1)}, u32[]{:S(2)}, u32[]{:S(2)}) async-start(bf16[4,208,128]{2,1,0:T(8,128)(2,1)} %get-tuple-element.14), calls=%async_computation | async-start | bytes 425984 | tf_op jit(solution)/shard_map/all_to_all | solution.py:251
  22.3 1.3 copy-start.9
  34.9 18.6 %all-to-all-start.1 = ((bf16[16,4,64,128]{3,2,1,0:T(8,128)(2,1)}), bf16[16,4,64,128]{3,2,1,0:T(8,128)(2,1)S(1)}, u32[]{:S(2)}, u32[]{:S(2)}) async-start(bf16[16,4,64,128]{3,2,1,0:T(8,128)(2,1)} %broadcast_in_dim.24), calls=%async_computation.1 | async-start | bytes 2097152 | tf_op jit(solution)/shard_map/all_to_all | solution.py:257
  41.7 22.5 %copy-start = (s32[256]{0:T(256)S(1)}, s32[256]{0:T(256)}, u32[]{:S(2)}) copy-start(s32[256]{0:T(256)} %param.14) | copy-start | bytes 3076
  45.9 1.9 %copy-start.7 = (bf16[2048,1024]{1,0:T(8,128)(2,1)}, bf16[2048,1024]{1,0:T(8,128)(2,1)S(1)}, u32[]{:S(2)}) copy-start(bf16[2048,1024]{1,0:T(8,128)(2,1)S(1)} %build_backward.1.adj_ref) | copy-start | bytes 12582916
  53.5 10.7 %collective-permute-start = (bf16[4096,128]{1,0:T(8,128)(2,1)S(1)}, bf16[4096,128]{1,0:T(8,128)(2,1)S(1)}, u32[]{:S(2)}, u32[]{:S(2)}) collective-permute-start(bf16[4096,128]{1,0:T(8,128)(2,1)S(1)} %bitcast.12), channel_id=1, source_target_pairs={{0,4},{4,0},{1,5},{5,1},{2,6},{6,2},{3,7},{7,3},{8,12},{12,8},{9,1... | collective-permute-start | bytes 3145736 | tf_op jit(solution)/shard_map/ppermute | solution.py:268
  64.2 1.6 %copy-start.10 = (bf16[256,4096]{1,0:T(8,128)(2,1)S(1)}, bf16[256,4096]{1,0:T(8,128)(2,1)}, u32[]{:S(2)}) copy-start(bf16[256,4096]{1,0:T(8,128)(2,1)} %copy-done.9) | copy-start | bytes 6291460
  65.8 13.2 %copy-start.1 = (bf16[512,512]{1,0:T(8,128)(2,1)S(1)}, bf16[512,512]{1,0:T(8,128)(2,1)}, u32[]{:S(2)}) copy-start(bf16[512,512]{1,0:T(8,128)(2,1)} %weight_ref.1) | copy-start | bytes 1572868
  65.8 13.2 %copy-start.4 = (bf16[64,512]{1,0:T(8,128)(2,1)S(1)}, bf16[64,512]{1,0:T(8,128)(2,1)}, u32[]{:S(2)}) copy-start(bf16[64,512]{1,0:T(8,128)(2,1)} %cot_ref.1) | copy-start | bytes 196612
  67.8 11.2 %all-to-all-start.2 = ((bf16[4,64,128]{2,1,0:T(8,128)(2,1)}), bf16[4,64,128]{2,1,0:T(8,128)(2,1)S(1)}, u32[]{:S(2)}, u32[]{:S(2)}) async-start(bf16[4,64,128]{2,1,0:T(8,128)(2,1)} %bitcast.8), calls=%async_computation.2 | async-start | bytes 131072 | tf_op jit(solution)/shard_map/all_to_all | solution.py:278
  119.0 10.2 %all-to-all-start.5 = ((bf16[4,16,128]{2,1,0:T(8,128)(2,1)}), bf16[4,16,128]{2,1,0:T(8,128)(2,1)S(1)}, u32[]{:S(2)}, u32[]{:S(2)}) async-start(bf16[4,16,128]{2,1,0:T(8,128)(2,1)} %sum_ring.1), calls=%async_computation.5 | async-start | bytes 32768 | tf_op jit(solution)/shard_map/all_to_all | solution.py:290
  124.7 2.2 %copy-start.8 = (bf16[2048,1024]{1,0:T(8,128)(2,1)S(1)}, bf16[2048,1024]{1,0:T(8,128)(2,1)}, u32[]{:S(2)}) copy-start(bf16[2048,1024]{1,0:T(8,128)(2,1)} %copy-done.7) | copy-start | bytes 12582916

commit v2 on v1

--- a/solution.py
+++ b/solution.py
@@ -18,17 +18,18 @@
 
 VMEM = pl.BlockSpec(memory_space=pltpu.VMEM)
 SMEM = pl.BlockSpec(memory_space=pltpu.SMEM)
-
-
-def call(kernel, out_shape, in_specs, scratch=(), micros=2, name=None):
+HBM = pl.BlockSpec(memory_space=pltpu.HBM)
+
+
+def call(kernel, out_shape, in_specs, scratch=(), micros=2, name=None, out_spec=VMEM, limit=24):
     single = not isinstance(out_shape, (tuple, list))
     return pl.pallas_call(
         kernel,
         out_shape=out_shape,
         in_specs=in_specs,
-        out_specs=VMEM if single else [VMEM] * len(out_shape),
+        out_specs=out_spec if single else [out_spec] * len(out_shape),
         scratch_shapes=list(scratch),
-        compiler_params=pltpu.CompilerParams(vmem_limit_bytes=24 * 1024 * 1024),
+        compiler_params=pltpu.CompilerParams(vmem_limit_bytes=limit * 1024 * 1024),
         cost_estimate=pl.CostEstimate(
             flops=int(micros * 1e9), bytes_accessed=int(micros * 1e6), transcendentals=0
         ),
@@ -78,33 +79,44 @@
     return jnp.where(values == 0.0, -1, row * TILE + col)
 
 
-def onehots(code):
-    row = code >> 7
-    col = code & (TILE - 1)
-    positions = lax.broadcasted_iota(jnp.int32, (TILE, code.shape[1]), 0)
-    one = jnp.float32(1.0)
-    zero = jnp.float32(0.0)
-    return (
-        jnp.where(positions == row, one, zero).astype(jnp.bfloat16),
-        jnp.where(positions == col, one, zero).astype(jnp.bfloat16),
-    )
+def onehot(index):
+    positions = lax.broadcasted_iota(jnp.int32, (TILE, index.shape[1]), 0)
+    return jnp.where(positions == index, jnp.float32(1.0), jnp.float32(0.0)).astype(jnp.bfloat16)
 
 
 def nt(left, right):
     return lax.dot_general(left, right, (((1,), (1,)), ((), ())), preferred_element_type=jnp.float32)
 
 
-def prepare(count_ref, feature_ref, degree_ref, slot_ref, edge_ref, out_ref, scale_ref):
-    scale = degree_scale(degree_ref[...])
+def start_copies(sems, *pairs):
+    copies = [pltpu.make_async_copy(source, target, sems.at[i]) for i, (source, target) in enumerate(pairs)]
+    for copy in copies:
+        copy.start()
+    return copies
+
+
+def slot_row(count, slots):
+    place = lax.broadcasted_iota(jnp.int32, (1, SLOTS), 1)
+    rest = jnp.where(lax.broadcasted_iota(jnp.int32, (1, TILE - SLOTS), 1) == 0, count, 0)
+    return jnp.concatenate([jnp.where(place < count, slots & 127, -1), rest], axis=1)
+
+
+def prepare(count_ref, feature_hbm, degree_hbm, slot_hbm, edge_hbm, out_ref, scale_ref, feature, degree, slot, edge, sems):
+    copies = start_copies(
+        sems, (degree_hbm, degree), (feature_hbm, feature), (slot_hbm, slot), (edge_hbm.at[0], edge)
+    )
+    count = count_ref[0]
+    copies[0].wait()
+    scale = degree_scale(degree[...])
     scale_ref[...] = scale
-    scaled = (feature_ref[...].astype(jnp.float32) * scale).astype(jnp.bfloat16)
-    count = count_ref[0]
-    live = lax.broadcasted_iota(jnp.int32, edge_ref.shape, 0) < count
-    codes = jnp.where(live, encode(edge_ref[...]), 0.0).astype(jnp.bfloat16)
-    used = lax.broadcasted_iota(jnp.int32, (1, SLOTS), 1) < count
-    slots = jnp.where(used, slot_ref[...], -1).astype(jnp.float32)
-    slots = jnp.concatenate([slots, jnp.zeros((1, TILE - SLOTS), jnp.float32)], axis=1)
-    slots = jnp.broadcast_to(slots, (16, TILE)).astype(jnp.bfloat16)
+    copies[1].wait()
+    scaled = (feature[...].astype(jnp.float32) * scale).astype(jnp.bfloat16)
+    copies[2].wait()
+    slots = slot_row(count, slot[...])
+    slots = jnp.broadcast_to(slots.astype(jnp.float32), (16, TILE)).astype(jnp.bfloat16)
+    copies[3].wait()
+    live = lax.broadcasted_iota(jnp.int32, edge.shape, 0) < count
+    codes = jnp.where(live, encode(edge[...]), 0.0).astype(jnp.bfloat16)
     for i in range(4):
         out_ref[i, 0:SUB, :] = scaled
         for p in range(4):
@@ -112,20 +124,33 @@
         out_ref[i, 192:208, :] = slots
 
 
-def build_forward(slot_ref, count_ref, edge_ref, wide_ref):
+def mark_edges(count_ref, slot_ref, edge_ref, code_ref):
+    count = count_ref[0]
+    row = jnp.broadcast_to(slot_row(count, slot_ref[...]), (8, TILE))
+    code_ref[SLOTS:SLOTS + 8, :] = jnp.concatenate([row] * 4, axis=1)
+    edges = edge_ref[0]
+    live = lax.broadcasted_iota(jnp.int32, edges.shape, 0) < count
+    code_ref[0:SLOTS, :] = jnp.where(live, edges, -1)
+
+
+def build_forward(slot_ref, core_ref, code_ref, wide_ref):
     wide_ref[...] = jnp.zeros_like(wide_ref)
-    count = count_ref[0]
-
-    def step(group, carry):
-        for k in range(4):
-            j = group * 4 + k
-            row, col = onehots(jnp.where(j < count, edge_ref[pl.ds(j, 1), :], -1))
-            tile = nt(row, col).astype(jnp.bfloat16)
-            row_at = pl.multiple_of((slot_ref[j] >> 6) * TILE, TILE)
-            wide_ref[pl.ds(row_at, TILE), pl.ds(pl.multiple_of(j * TILE, TILE), TILE)] = tile
-        return carry
-
-    lax.fori_loop(0, (count + 3) >> 2, step, 0)
+    first = core_ref[0] * SUB
+    for b in range(2):
+
+        def step(group, carry):
+            for k in range(4):
+                j = group * 4 + k
+                code = code_ref[b, pl.ds(j, 1), :]
+                col = (code & (TILE - 1)) - first
+                col = jnp.where(jnp.logical_and(col >= 0, col < SUB), col + (k % 2) * SUB, -1)
+                tile = nt(onehot(code >> 7), onehot(col)).astype(jnp.bfloat16)
+                row_at = pl.multiple_of(((slot_ref[b, j] >> 6) & 1) * TILE, TILE)
+                lane = pl.multiple_of((group * 2 + k // 2) * TILE, TILE)
+                wide_ref[b, pl.ds(row_at, TILE), pl.ds(lane, TILE)] += tile
+            return carry
+
+        lax.fori_loop(0, (slot_ref[b, SLOTS] + 3) >> 2, step, 0)
 
 
 def build_backward(slot_ref, quarter_ref, ring_ref, out_ref, list_ref, code_ref):
@@ -155,8 +180,7 @@
             block = i >> 5
             at = block * TILE + (i & 31)
             code = jnp.concatenate([code_ref[pl.ds(at + p * SLOTS, 1), :] for p in range(4)], axis=1)
-            row, col = onehots(code)
-            tile = nt(col, row).astype(jnp.bfloat16)
+            tile = nt(onehot(code & (TILE - 1)), onehot(code >> 7)).astype(jnp.bfloat16)
             at = pl.multiple_of((slot & 15) * TILE, TILE)
             lane = pl.multiple_of((block * 2 + (slot >> 6)) * TILE, TILE)
             out_ref[pl.ds(at, TILE), pl.ds(lane, TILE)] = tile
@@ -165,22 +189,22 @@
     lax.fori_loop(0, (found + 3) >> 2, step, 0)
 
 
-def aggregate(slot_ref, core_ref, wide_ref, own_ref, other_ref, degree_ref, out_ref, picked):
-    core = core_ref[0]
-    for j in range(SLOTS):
-        tile = slot_ref[j] & 63
-        at = pl.multiple_of(((tile & 15) * 4 + (tile >> 4)) * SUB, SUB)
-        own_at = pl.multiple_of(j * TILE + core * SUB, SUB)
-        other_at = pl.multiple_of(j * TILE + (1 - core) * SUB, SUB)
-        picked[pl.ds(own_at, SUB), :] = own_ref[pl.ds(at, SUB), :]
-        picked[pl.ds(other_at, SUB), :] = other_ref[pl.ds(at, SUB), :]
-    total = jnp.dot(wide_ref[...], picked[...], preferred_element_type=jnp.float32)
-    out_ref[...] = (total * degree_scale(degree_ref[...])).astype(jnp.bfloat16)
+def aggregate(slot_ref, wide_ref, source_ref, out_ref, picked):
+    for b in range(2):
+        for j in range(SLOTS):
+            tile = slot_ref[b, j] & 63
+            at = pl.multiple_of(((tile & 15) * 4 + (tile >> 4)) * SUB, SUB)
+            picked[b, j * SUB:(j + 1) * SUB, :] = source_ref[pl.ds(at, SUB), :]
+        total = jnp.dot(wide_ref[b], picked[b], preferred_element_type=jnp.float32)
+        for k in range(4):
+            out_ref[b * 4 + k] = total[k * SUB:(k + 1) * SUB, :]
 
 
 def dense(part_ref, panel_ref, weight_ref, cot_ref, degree_ref, act_ref, spread_ref, term_ref):
     scale = degree_scale(degree_ref[pl.ds(part_ref[0], 1), :])
-    rows = jnp.concatenate([panel_ref[p] for p in range(4)], axis=1)
+    rows = jnp.concatenate(
+        [((panel_ref[p] + panel_ref[p + 4]) * scale).astype(jnp.bfloat16) for p in range(4)], axis=1
+    )
     pre_act = jnp.dot(rows, weight_ref[...], preferred_element_type=jnp.float32)
     output, slope = gelu_parts(pre_act)
     act_ref[...] = output.astype(jnp.bfloat16)
@@ -215,11 +239,11 @@
 def spread_back(adj_ref, ring_ref, out_ref, grad):
     for i in range(16):
         grad[i * SUB:(i + 1) * SUB, :] = ring_ref[i, 0:SUB, :]
-    for block in range(8):
-        rows = adj_ref[block * 256:(block + 1) * 256, :]
+    for i in range(8):
+        rows = adj_ref[i * 256:(i + 1) * 256, :]
         terms = jnp.dot(rows, grad[...], preferred_element_type=jnp.float32).astype(jnp.bfloat16)
         for k in range(4):
-            out_ref[block * 4 + k] = terms[k * SUB:(k + 1) * SUB, :]
+            out_ref[i * 4 + k] = terms[k * SUB:(k + 1) * SUB, :]
 
 
 def finish(plane_ref, scale_ref, feature_ref, weight_ref):
@@ -238,23 +262,63 @@
     bf16 = jnp.bfloat16
     shape = jax.ShapeDtypeStruct
     zh, core, zl = lax.axis_index("zh"), lax.axis_index("c"), lax.axis_index("zl")
-    slots = jnp.clip(tile_slot, 0, 127)
-    edges = tile_edges[0]
 
     piece, src_scale = call(
         prepare,
         (shape((4, 208, TILE), bf16), shape((SUB, 1), jnp.float32)),
-        [SMEM, VMEM, VMEM, VMEM, VMEM],
+        [SMEM, HBM, HBM, HBM, HBM],
+        [
+            pltpu.VMEM((SUB, TILE), bf16),
+            pltpu.VMEM((1, SUB), jnp.int32),
+            pltpu.VMEM((1, SLOTS), jnp.int32),
+            pltpu.VMEM((SLOTS, 512), jnp.int32),
+            pltpu.SemaphoreType.DMA((4,)),
+        ],
         micros=1,
         name="prepare",
-    )(tile_count, features, deg_src[None], slots, edges)
-    piece = lax.all_to_all(piece, "zh", 0, 0)
-    wide = call(build_forward, shape((NB, SLOTS * TILE), bf16), [SMEM, SMEM, VMEM], micros=6, name="build_forward")(
-        slots[0], tile_count, edges
-    )
-    piece, wide = lax.optimization_barrier((piece, wide))
-
-    plane_sources = lax.all_to_all(jnp.broadcast_to(piece[:, :SUB], (16, 4, SUB, TILE)), ("x", "y"), 0, 0)
+        limit=62,
+    )(tile_count, features, deg_src[None], tile_slot, tile_edges)
+    code = call(
+        mark_edges,
+        shape((SLOTS + 8, 512), jnp.int32),
+        [SMEM, VMEM, VMEM],
+        micros=1,
+        name="mark_edges",
+    )(tile_count, tile_slot, tile_edges)
+    ring_piece = lax.all_to_all(piece, "zh", 0, 0)
+    codes = lax.all_gather(code, "c")
+    slots = codes[:, SLOTS, :TILE]
+    ring_piece, codes = lax.optimization_barrier((ring_piece, codes))
+
+    plane_sources = lax.all_to_all(jnp.broadcast_to(ring_piece[:, :SUB], (16, 4, SUB, TILE)), ("x", "y"), 0, 0)
+    wide = call(
+        build_forward,
+        shape((2, NB, SLOTS * SUB), bf16),
+        [SMEM, SMEM, VMEM],
+        micros=6,
+        name="build_forward",
+    )(slots, core[None], codes)
+    plane_sources, wide = lax.optimization_barrier((plane_sources, wide))
+
+    partial = call(
+        aggregate,
+        shape((8, SUB, TILE), jnp.float32),
+        [SMEM, VMEM, VMEM],
+        [pltpu.VMEM((2, SLOTS * SUB, TILE), bf16)],
+        name="aggregate",
+    )(slots, wide, plane_sources.reshape(64 * SUB, TILE))
+
+    panels = lax.all_to_all(partial, ("c", "zl"), 0, 0)
+    activated, spread, terms = call(
+        dense,
+        (shape((SUB, 512), bf16), shape((4, SUB, TILE), bf16), shape((512, 512), bf16)),
+        [SMEM] + [VMEM] * 4,
+        name="dense",
+    )(zl[None], panels, weight, cotangent, deg_dst.reshape(4, SUB))
+
+    parts = lax.all_to_all(terms.reshape(32, 16, 512), PLANE, 0, 0)
+    ring = call(pack_ring, shape((16, SUB + 16, TILE), bf16), [VMEM] * 2, name="pack_ring")(parts, spread)
+    ring = lax.all_to_all(ring, RING, 0, 0)
     adjacent = call(
         build_backward,
         shape((2048, 1024), bf16),
@@ -262,30 +326,8 @@
         [pltpu.SMEM((4 * SLOTS + 8,), jnp.int32), pltpu.VMEM((4 * TILE, TILE), jnp.int32)],
         micros=6,
         name="build_backward",
-    )(piece[:, 192, :SLOTS].astype(jnp.int32).reshape(4 * SLOTS), zh[None], piece)
-    own_sources = plane_sources.reshape(64 * SUB, TILE)
-    own_sources, adjacent = lax.optimization_barrier((own_sources, adjacent))
-    other_sources = lax.ppermute(own_sources, "c", [(0, 1), (1, 0)])
-
-    aggregated = call(
-        aggregate,
-        shape((NB, TILE), bf16),
-        [SMEM, SMEM, VMEM, VMEM, VMEM, VMEM],
-        [pltpu.VMEM((SLOTS * TILE, TILE), bf16)],
-        name="aggregate",
-    )(slots[0], core[None], wide, own_sources, other_sources, deg_dst[None])
-
-    panels = lax.all_to_all(aggregated.reshape(4, SUB, TILE), "zl", 0, 0)
-    activated, spread, terms = call(
-        dense,
-        (shape((SUB, 512), bf16), shape((4, SUB, TILE), bf16), shape((512, 512), bf16)),
-        [SMEM] + [VMEM] * 4,
-        name="dense",
-    )(zl[None], panels, weight, cotangent, deg_dst.reshape(4, SUB))
-
-    parts = lax.all_to_all(terms.reshape(32, 16, 512), PLANE, 0, 0)
-    ring = call(pack_ring, shape((16, SUB + 16, TILE), bf16), [VMEM] * 2, name="pack_ring")(parts, spread)
-    ring = lax.all_to_all(ring, RING, 0, 0)
+    )(ring_piece[:, 192, :SLOTS].astype(jnp.int32).reshape(4 * SLOTS), zh[None], ring_piece)
+    ring, adjacent = lax.optimization_barrier((ring, adjacent))
     panel_sum = call(sum_ring, shape((4, 16, TILE), bf16), [VMEM], micros=1, name="sum_ring")(ring)
     weight_rows = lax.all_to_all(panel_sum, "zl", 0, 0).reshape(SUB, TILE)
     source_terms = call(

time: 155 us -> 153 us (0.987)
  blocking collectives: 61.7 us -> 41 us
  waiting for transfers between devices: 23.4 us -> 40.4 us
  Pallas kernels: 12.7 us -> 15.1 us
  local copies, waits for them, and re-layouts: 10.8 us -> 8.58 us
  starting transfers between devices: 43.1 us -> 45.3 us
    all_to_all x1 -> x0, blocking collectives: 21.7 us -> none  [local(): ring = lax.all_to_all(ring, RING, 0, 0)]
    all_to_all x3 -> x4, waiting for transfers between devices: 20.1 us -> 39.4 us  [the longest x1 12.3 us: local(): ring = lax.all_to_all(ring, RING, 0, 0)]
    all_to_all x3 -> x4, starting transfers between devices: 29 us -> 39.6 us  [the longest x1 15.6 us: local(): ring_piece = lax.all_to_all(piece, 'zh', 0, 0)]
    ppermute x1 -> x0, starting transfers between devices: 8.44 us -> none  [local(): other_sources = lax.ppermute(own_sources, 'c', [(0, 1), (1, 0)])]
    all_gather x0 -> x1, blocking collectives: none -> 2.51 us  [local(): codes = lax.all_gather(code, 'c')]
    ppermute x1 -> x0, waiting for transfers between devices: 2.26 us -> none  [local(): other_sources = lax.ppermute(own_sources, 'c', [(0, 1), (1, 0)])]
    unnamed x22 -> x20, local copies, waits for them, and re-layouts: 9.28 us -> 7.07 us
    pallas_call x2 -> x3, Pallas kernels: 3.69 us -> 4.76 us  [the longest x1 2.71 us: local(): call(build_forward, shape((2, NB, SLOTS * SUB), bf16), [SMEM, SMEM, VMEM]...]
where the time goes in v2:
time: 153 us; the launch traced here: 152 us
  starting transfers between devices  45.3 us (30%)
  blocking collectives  41 us (27%)
  waiting for transfers between devices  40.4 us (26%)
  Pallas kernels  15.1 us (10%)
  local copies, waits for them, and re-layouts  8.58 us (6%)
    all_to_all x1, blocking collectives, local(): plane = lax.all_to_all(plane, PLANE, 0, 0)  23.3 us
    all_to_all x1, starting transfers between devices, local(): ring_piece = lax.all_to_all(piece, 'zh', 0, 0)  15.6 us
    all_to_all x1, blocking collectives, local(): parts = lax.all_to_all(terms.reshape(32, 16, 512), PLANE, 0, 0)  15.2 us
    all_to_all x1, starting transfers between devices, local(): panels = lax.all_to_all(partial, ('c', 'zl'), 0, 0)  13.4 us
    all_to_all x1, waiting for transfers between devices, local(): ring = lax.all_to_all(ring, RING, 0, 0)  12.3 us
    all_to_all x1, waiting for transfers between devices, local(): ring_piece = lax.all_to_all(piece, 'zh', 0, 0)  10.4 us
    all_to_all x1, waiting for transfers between devices, local(): panels = lax.all_to_all(partial, ('c', 'zl'), 0, 0)  8.97 us
    all_to_all x1, waiting for transfers between devices, local(): lax.all_to_all(jnp.broadcast_to(ring_piece[:, :SUB], (16, 4, SUB, TILE)),...  7.78 us
  transfers between devices with their start and end apart: 5, of which 5 were waited for; matrix products, arithmetic and copies ran while one was open for 0% of the time, Pallas kernels for 5%

profile of v2, /device:TPU:1, one launch (start us, length us, event | category | flops | bytes accessed | tf_op | source)
XLA Modules:
  0.0 151.9 jit_solution(10175612408917888712)
XLA Ops:
  0.6 0.0 copy-start.1
  0.6 0.0 copy-start.3
  1.3 1.7 %prepare.1 = (bf16[4,208,128]{2,1,0:T(8,128)(2,1)}, f32[64,1]{1,0:T(8,128)}) custom-call(s32[1]{0:T(128)S(6)} %copy.14.count_ref, bf16[64,128]{1,0:T(8,128)(2,1)} %feature_hbm.1, s32[1,64]{1,0:T(1,128)} %bitcast.18, s32[1,32]{1,0:T(1,128)} %slot_hbm.1, s32[1,32,512]{2,1,0:T(8,128)} %edge_hbm.1), custom_call_target="tpu_custom_call" | custom-call | flops 1000000000 | bytes 1000000 | tf_op jit(solution)/shard_map/prepare/pallas_call | solution.py:266
  3.0 15.6 %all-to-all-start = ((bf16[4,208,128]{2,1,0:T(8,128)(2,1)}), bf16[4,208,128]{2,1,0:T(8,128)(2,1)S(1)}, u32[]{:S(2)}, u32[]{:S(2)}) async-start(bf16[4,208,128]{2,1,0:T(8,128)(2,1)} %get-tuple-element.16), calls=%async_computation | async-start | bytes 425984 | tf_op jit(solution)/shard_map/all_to_all | solution.py:288
  18.7 0.0 copy-done.1
  18.7 0.0 copy-done.3
  18.7 0.1 mark_edges.1
  18.8 2.5 %all-gather = s32[80,512]{1,0:T(8,128)S(1)} all-gather(s32[40,512]{1,0:T(8,128)S(1)} %mark_edges.1), channel_id=2, replica_groups=mesh['zh'=4,'x'=4,'y'=4,'c'=2,'zl'=4] {'c'}, dimensions={0}, use_global_device_ids=true | all-gather | bytes 245760 | tf_op jit(solution)/shard_map/all_gather | solution.py:289
  21.3 10.4 %all-to-all-done.ring_ref = bf16[4,208,128]{2,1,0:T(8,128)(2,1)S(1)} async-done(((bf16[4,208,128]{2,1,0:T(8,128)(2,1)}), bf16[4,208,128]{2,1,0:T(8,128)(2,1)S(1)}, u32[]{:S(2)}, u32[]{:S(2)}) %all-to-all-start) | async-done | bytes 213024 | tf_op jit(solution)/shard_map/all_to_all | solution.py:288
  31.7 1.2 broadcast_in_dim.20
  32.9 6.8 %all-to-all-start.1 = ((bf16[16,4,64,128]{3,2,1,0:T(8,128)(2,1)}), bf16[16,4,64,128]{3,2,1,0:T(8,128)(2,1)S(1)}, u32[]{:S(2)}, u32[]{:S(2)}) async-start(bf16[16,4,64,128]{3,2,1,0:T(8,128)(2,1)} %broadcast_in_dim.20), calls=%async_computation.1 | async-start | bytes 2097152 | tf_op jit(solution)/shard_map/all_to_all | solution.py:293
  39.7 2.7 %build_forward.1.wide_ref = bf16[2,256,2048]{2,1,0:T(8,128)(2,1)S(1)} custom-call(s32[2,128]{1,0:T(2,128)S(1)} %bitcast.15, s32[1]{0:T(128)} %bitcast.4.core_ref, s32[2,40,512]{2,1,0:T(8,128)S(1)} %bitcast.14), custom_call_target="tpu_custom_call" | custom-call | flops 6000000000 | bytes 6000000 | tf_op jit(solution)/shard_map/build_forward/pallas_call | solution.py:294
  42.4 0.0 copy-start.6
  42.4 1.3 copy-done.6
  43.7 7.8 %all-to-all-done.1 = bf16[16,4,64,128]{3,2,1,0:T(8,128)(2,1)S(1)} async-done(((bf16[16,4,64,128]{3,2,1,0:T(8,128)(2,1)}), bf16[16,4,64,128]{3,2,1,0:T(8,128)(2,1)S(1)}, u32[]{:S(2)}, u32[]{:S(2)}) %all-to-all-start.1) | async-done | bytes 1048608 | tf_op jit(solution)/shard_map/all_to_all | solution.py:293
  51.5 0.0 copy-start.7
  51.5 1.6 %copy-done.7 = bf16[2,256,2048]{2,1,0:T(8,128)(2,1)S(1)} copy-done((bf16[2,256,2048]{2,1,0:T(8,128)(2,1)S(1)}, bf16[2,256,2048]{2,1,0:T(8,128)(2,1)}, u32[]{:S(2)}) %copy-start.7) | copy-done | bytes 2097176
  53.1 0.0 copy-start.9
  53.1 0.0 copy-start
  53.1 0.0 copy-start.2
  53.1 2.0 %aggregate.1 = f32[8,64,128]{2,1,0:T(8,128)} custom-call(s32[2,128]{1,0:T(2,128)S(1)} %bitcast.16, bf16[2,256,2048]{2,1,0:T(8,128)(2,1)S(1)} %copy-done.7, bf16[4096,128]{1,0:T(8,128)(2,1)S(1)} %bitcast.11), custom_call_target="tpu_custom_call" | custom-call | flops 2000000000 | bytes 2000000 | tf_op jit(solution)/shard_map/aggregate/pallas_call | solution.py:303
  55.1 13.4 %all-to-all-start.2 = ((f32[8,64,128]{2,1,0:T(8,128)}), f32[8,64,128]{2,1,0:T(8,128)S(1)}, u32[]{:S(2)}, u32[]{:S(2)}) async-start(f32[8,64,128]{2,1,0:T(8,128)} %aggregate.1), calls=%async_computation.2 | async-start | bytes 524288 | tf_op jit(solution)/shard_map/all_to_all | solution.py:311
  68.5 0.0 copy-done.9
  68.5 0.1 reshape.23.degree_ref
  68.6 9.0 %all-to-all-done.2.panel_ref = f32[8,64,128]{2,1,0:T(8,128)S(1)} async-done(((f32[8,64,128]{2,1,0:T(8,128)}), f32[8,64,128]{2,1,0:T(8,128)S(1)}, u32[]{:S(2)}, u32[]{:S(2)}) %all-to-all-start.2) | async-done | bytes 262176 | tf_op jit(solution)/shard_map/all_to_all | solution.py:311
  77.6 0.0 copy-done
  77.6 0.0 copy-done.2
  77.6 1.0 dense.1
  78.6 15.2 %all_to_all.35.part_ref = bf16[32,16,512]{2,1,0:T(8,128)(2,1)S(1)} all-to-all(bf16[32,16,512]{2,1,0:T(8,128)(2,1)S(1)} %bitcast.12), channel_id=1, replica_groups=mesh['zh'=4,'x'=4,'y'=4,'c'=2,'zl'=4] {'x','y','c'}, dimensions={0} | all-to-all | bytes 1048576 | tf_op jit(solution)/shard_map/all_to_all | solution.py:319
  93.7 0.8 pack_ring.1
  94.6 3.7 %all-to-all-start.4 = ((bf16[16,80,128]{2,1,0:T(8,128)(2,1)}), bf16[16,80,128]{2,1,0:T(8,128)(2,1)S(1)}, u32[]{:S(2)}, u32[]{:S(2)}) async-start(bf16[16,80,128]{2,1,0:T(8,128)(2,1)} %pack_ring.1), calls=%async_computation.4 | async-start | bytes 655360 | tf_op jit(solution)/shard_map/all_to_all | solution.py:321
  98.3 0.1 reshape.26.slot_ref
  98.4 3.8 %build_backward.1.adj_ref = bf16[2048,1024]{1,0:T(8,128)(2,1)S(1)} custom-call(s32[128]{0:T(128)S(1)} %reshape.26.slot_ref, s32[1]{0:T(128)} %bitcast.7.quarter_ref, bf16[4,208,128]{2,1,0:T(8,128)(2,1)S(1)} %all-to-all-done.ring_ref), custom_call_target="tpu_custom_call" | custom-call | flops 6000000000 | bytes 6000000 | tf_op jit(solution)/shard_map/build_backward/pallas_call | solution.py:322
  102.2 0.0 copy-start.4
  102.2 1.9 %copy-done.4 = bf16[2048,1024]{1,0:T(8,128)(2,1)} copy-done((bf16[2048,1024]{1,0:T(8,128)(2,1)}, bf16[2048,1024]{1,0:T(8,128)(2,1)S(1)}, u32[]{:S(2)}) %copy-start.4) | copy-done | bytes 4194328
  104.2 12.3 %all-to-all-done.4.ring_ref = bf16[16,80,128]{2,1,0:T(8,128)(2,1)S(1)} async-done(((bf16[16,80,128]{2,1,0:T(8,128)(2,1)}), bf16[16,80,128]{2,1,0:T(8,128)(2,1)S(1)}, u32[]{:S(2)}, u32[]{:S(2)}) %all-to-all-start.4) | async-done | bytes 327712 | tf_op jit(solution)/shard_map/all_to_all | solution.py:321
  116.4 0.6 sum_ring.1
  117.1 5.8 %all-to-all-start.5 = ((bf16[4,16,128]{2,1,0:T(8,128)(2,1)}), bf16[4,16,128]{2,1,0:T(8,128)(2,1)S(1)}, u32[]{:S(2)}, u32[]{:S(2)}) async-start(bf16[4,16,128]{2,1,0:T(8,128)(2,1)} %sum_ring.1), calls=%async_computation.5 | async-start | bytes 32768 | tf_op jit(solution)/shard_map/all_to_all | solution.py:332
  122.8 0.0 copy-start.5
  122.8 2.2 %copy-done.5 = bf16[2048,1024]{1,0:T(8,128)(2,1)S(1)} copy-done((bf16[2048,1024]{1,0:T(8,128)(2,1)S(1)}, bf16[2048,1024]{1,0:T(8,128)(2,1)}, u32[]{:S(2)}) %copy-start.5) | copy-done | bytes 4194328
  125.0 1.3 spread_back.1
  126.3 1.0 all-to-all-done.5
  127.3 0.1 broadcast_in_dim.23
  127.4 0.0 copy-start.8
  127.4 0.1 pad_maximum_fusion
  127.5 23.3 %all_to_all.36.plane_ref = bf16[32,128,128]{2,1,0:T(8,128)(2,1)S(1)} all-to-all(bf16[32,128,128]{2,1,0:T(8,128)(2,1)S(1)} %pad_maximum_fusion), channel_id=1, replica_groups=mesh['zh'=4,'x'=4,'y'=4,'c'=2,'zl'=4] {'x','y','c'}, dimensions={0} | all-to-all | bytes 2097152 | tf_op jit(solution)/shard_map/all_to_all | solution.py:341
  150.8 0.0 copy-done.8
  150.8 1.1 finish.1
  (3 shorter events, 0.0 us)
Async XLA Ops:
  0.6 18.0 %copy-start.1 = (s32[1,32,512]{2,1,0:T(8,128)S(1)}, s32[1,32,512]{2,1,0:T(8,128)}, u32[]{:S(2)}) copy-start(s32[1,32,512]{2,1,0:T(8,128)} %edge_hbm.1) | copy-start | bytes 196612
  0.6 18.0 %copy-start.3 = (s32[1,32]{1,0:T(1,128)S(1)}, s32[1,32]{1,0:T(1,128)}, u32[]{:S(2)}) copy-start(s32[1,32]{1,0:T(1,128)} %slot_hbm.1) | copy-start | bytes 388
  3.0 28.6 %all-to-all-start = ((bf16[4,208,128]{2,1,0:T(8,128)(2,1)}), bf16[4,208,128]{2,1,0:T(8,128)(2,1)S(1)}, u32[]{:S(2)}, u32[]{:S(2)}) async-start(bf16[4,208,128]{2,1,0:T(8,128)(2,1)} %get-tuple-element.16), calls=%async_computation | async-start | bytes 425984 | tf_op jit(solution)/shard_map/all_to_all | solution.py:288
  32.9 18.6 %all-to-all-start.1 = ((bf16[16,4,64,128]{3,2,1,0:T(8,128)(2,1)}), bf16[16,4,64,128]{3,2,1,0:T(8,128)(2,1)S(1)}, u32[]{:S(2)}, u32[]{:S(2)}) async-start(bf16[16,4,64,128]{3,2,1,0:T(8,128)(2,1)} %broadcast_in_dim.20), calls=%async_computation.1 | async-start | bytes 2097152 | tf_op jit(solution)/shard_map/all_to_all | solution.py:293
  42.4 1.3 copy-start.6
  51.5 1.6 %copy-start.7 = (bf16[2,256,2048]{2,1,0:T(8,128)(2,1)S(1)}, bf16[2,256,2048]{2,1,0:T(8,128)(2,1)}, u32[]{:S(2)}) copy-start(bf16[2,256,2048]{2,1,0:T(8,128)(2,1)} %copy-done.6) | copy-start | bytes 6291460
  53.1 15.4 %copy-start.9 = (s32[256]{0:T(256)S(1)}, s32[256]{0:T(256)}, u32[]{:S(2)}) copy-start(s32[256]{0:T(256)} %param.14) | copy-start | bytes 3076
  53.1 24.5 %copy-start = (bf16[512,512]{1,0:T(8,128)(2,1)S(1)}, bf16[512,512]{1,0:T(8,128)(2,1)}, u32[]{:S(2)}) copy-start(bf16[512,512]{1,0:T(8,128)(2,1)} %weight_ref.1) | copy-start | bytes 1572868
  53.1 24.5 %copy-start.2 = (bf16[64,512]{1,0:T(8,128)(2,1)S(1)}, bf16[64,512]{1,0:T(8,128)(2,1)}, u32[]{:S(2)}) copy-start(bf16[64,512]{1,0:T(8,128)(2,1)} %cot_ref.1) | copy-start | bytes 196612
  55.1 22.5 %all-to-all-start.2 = ((f32[8,64,128]{2,1,0:T(8,128)}), f32[8,64,128]{2,1,0:T(8,128)S(1)}, u32[]{:S(2)}, u32[]{:S(2)}) async-start(f32[8,64,128]{2,1,0:T(8,128)} %aggregate.1), calls=%async_computation.2 | async-start | bytes 524288 | tf_op jit(solution)/shard_map/all_to_all | solution.py:311
  94.6 21.9 %all-to-all-start.4 = ((bf16[16,80,128]{2,1,0:T(8,128)(2,1)}), bf16[16,80,128]{2,1,0:T(8,128)(2,1)S(1)}, u32[]{:S(2)}, u32[]{:S(2)}) async-start(bf16[16,80,128]{2,1,0:T(8,128)(2,1)} %pack_ring.1), calls=%async_computation.4 | async-start | bytes 655360 | tf_op jit(solution)/shard_map/all_to_all | solution.py:321
  102.2 1.9 %copy-start.4 = (bf16[2048,1024]{1,0:T(8,128)(2,1)}, bf16[2048,1024]{1,0:T(8,128)(2,1)S(1)}, u32[]{:S(2)}) copy-start(bf16[2048,1024]{1,0:T(8,128)(2,1)S(1)} %build_backward.1.adj_ref) | copy-start | bytes 12582916
  117.1 10.2 %all-to-all-start.5 = ((bf16[4,16,128]{2,1,0:T(8,128)(2,1)}), bf16[4,16,128]{2,1,0:T(8,128)(2,1)S(1)}, u32[]{:S(2)}, u32[]{:S(2)}) async-start(bf16[4,16,128]{2,1,0:T(8,128)(2,1)} %sum_ring.1), calls=%async_computation.5 | async-start | bytes 32768 | tf_op jit(solution)/shard_map/all_to_all | solution.py:332
  122.8 2.2 %copy-start.5 = (bf16[2048,1024]{1,0:T(8,128)(2,1)S(1)}, bf16[2048,1024]{1,0:T(8,128)(2,1)}, u32[]{:S(2)}) copy-start(bf16[2048,1024]{1,0:T(8,128)(2,1)} %copy-done.4) | copy-start | bytes 12582916
  127.4 23.4 %copy-start.8 = (f32[64,1]{1,0:T(8,128)S(1)}, f32[64,1]{1,0:T(8,128)}, u32[]{:S(2)}) copy-start(f32[64,1]{1,0:T(8,128)} %get-tuple-element.26.scale_ref) | copy-start | bytes 772

commit v3 on v2

--- a/solution.py
+++ b/solution.py
@@ -13,7 +13,6 @@
 CUBIC = 0.044715
 ROWS = ("zh", "x", "y", "c")
 PLANE = ("x", "y", "c")
-RING = ("zh", "zl")
 FINE = (("zh", 4), ("x", 4), ("y", 4), ("c", 2), ("zl", 4))
 
 VMEM = pl.BlockSpec(memory_space=pltpu.VMEM)
@@ -117,11 +116,10 @@
     copies[3].wait()
     live = lax.broadcasted_iota(jnp.int32, edge.shape, 0) < count
     codes = jnp.where(live, encode(edge[...]), 0.0).astype(jnp.bfloat16)
-    for i in range(4):
-        out_ref[i, 0:SUB, :] = scaled
-        for p in range(4):
-            out_ref[i, SUB + p * SLOTS:SUB + (p + 1) * SLOTS, :] = codes[:, p * TILE:(p + 1) * TILE]
-        out_ref[i, 192:208, :] = slots
+    out_ref[0:SUB, :] = scaled
+    for p in range(4):
+        out_ref[SUB + p * SLOTS:SUB + (p + 1) * SLOTS, :] = codes[:, p * TILE:(p + 1) * TILE]
+    out_ref[192:208, :] = slots
 
 
 def mark_edges(count_ref, slot_ref, edge_ref, code_ref):
@@ -216,34 +214,37 @@
     term_ref[...] = terms.astype(jnp.bfloat16)
 
 
-def pack_ring(part_ref, spread_ref, out_ref):
-    total = part_ref[0].astype(jnp.float32)
-    for s in range(1, part_ref.shape[0]):
-        total = total + part_ref[s].astype(jnp.float32)
-    total = total.astype(jnp.bfloat16)
-    for i in range(16):
-        p = i % 4
-        out_ref[i, 0:SUB, :] = spread_ref[p]
-        out_ref[i, SUB:SUB + 16, :] = total[:, p * TILE:(p + 1) * TILE]
-
-
-def sum_ring(ring_ref, out_ref):
-    total = jnp.zeros((16, TILE), jnp.float32)
-    for i in range(16):
-        total = total + ring_ref[i, SUB:SUB + 16, :].astype(jnp.float32)
-    total = total.astype(jnp.bfloat16)
+def sum_first(ref, first=0, last=None):
+    total = ref[0, first:last].astype(jnp.float32)
+    for s in range(1, ref.shape[0]):
+        total = total + ref[s, first:last].astype(jnp.float32)
+    return total.astype(jnp.bfloat16)
+
+
+def pack_panels(part_ref, spread_ref, out_ref):
+    total = sum_first(part_ref)
+    piece = jnp.concatenate([total[:, p * TILE:(p + 1) * TILE] for p in range(4)], axis=0)
+    for p in range(4):
+        out_ref[p, 0:SUB, :] = spread_ref[p]
+        out_ref[p, SUB:TILE, :] = piece
+
+
+def merge_panels(panel_ref, out_ref):
     for i in range(4):
-        out_ref[i] = total
+        out_ref[i * SUB:(i + 1) * SUB, :] = panel_ref[i, 0:SUB, :]
+    out_ref[NB:NB + SUB, :] = sum_first(panel_ref, SUB, TILE)
 
 
 def spread_back(adj_ref, ring_ref, out_ref, grad):
-    for i in range(16):
-        grad[i * SUB:(i + 1) * SUB, :] = ring_ref[i, 0:SUB, :]
+    for i in range(4):
+        grad[i * NB:(i + 1) * NB, :] = ring_ref[i, 0:NB, :]
+    piece = sum_first(ring_ref, NB, NB + SUB)
     for i in range(8):
         rows = adj_ref[i * 256:(i + 1) * 256, :]
         terms = jnp.dot(rows, grad[...], preferred_element_type=jnp.float32).astype(jnp.bfloat16)
         for k in range(4):
-            out_ref[i * 4 + k] = terms[k * SUB:(k + 1) * SUB, :]
+            out_ref[i * 4 + k, 0:SUB, :] = terms[k * SUB:(k + 1) * SUB, :]
+            out_ref[i * 4 + k, SUB:TILE, :] = piece
 
 
 def finish(plane_ref, scale_ref, feature_ref, weight_ref):
@@ -265,7 +266,7 @@
 
     piece, src_scale = call(
         prepare,
-        (shape((4, 208, TILE), bf16), shape((SUB, 1), jnp.float32)),
+        (shape((208, TILE), bf16), shape((SUB, 1), jnp.float32)),
         [SMEM, HBM, HBM, HBM, HBM],
         [
             pltpu.VMEM((SUB, TILE), bf16),
@@ -285,10 +286,9 @@
         micros=1,
         name="mark_edges",
     )(tile_count, tile_slot, tile_edges)
-    ring_piece = lax.all_to_all(piece, "zh", 0, 0)
+    ring_piece = lax.all_gather(piece, "zh")
     codes = lax.all_gather(code, "c")
     slots = codes[:, SLOTS, :TILE]
-    ring_piece, codes = lax.optimization_barrier((ring_piece, codes))
 
     plane_sources = lax.all_to_all(jnp.broadcast_to(ring_piece[:, :SUB], (16, 4, SUB, TILE)), ("x", "y"), 0, 0)
     wide = call(
@@ -317,8 +317,6 @@
     )(zl[None], panels, weight, cotangent, deg_dst.reshape(4, SUB))
 
     parts = lax.all_to_all(terms.reshape(32, 16, 512), PLANE, 0, 0)
-    ring = call(pack_ring, shape((16, SUB + 16, TILE), bf16), [VMEM] * 2, name="pack_ring")(parts, spread)
-    ring = lax.all_to_all(ring, RING, 0, 0)
     adjacent = call(
         build_backward,
         shape((2048, 1024), bf16),
@@ -327,17 +325,18 @@
         micros=6,
         name="build_backward",
     )(ring_piece[:, 192, :SLOTS].astype(jnp.int32).reshape(4 * SLOTS), zh[None], ring_piece)
-    ring, adjacent = lax.optimization_barrier((ring, adjacent))
-    panel_sum = call(sum_ring, shape((4, 16, TILE), bf16), [VMEM], micros=1, name="sum_ring")(ring)
-    weight_rows = lax.all_to_all(panel_sum, "zl", 0, 0).reshape(SUB, TILE)
-    source_terms = call(
+    parts, adjacent = lax.optimization_barrier((parts, adjacent))
+    panels = call(pack_panels, shape((4, TILE, TILE), bf16), [VMEM] * 2, micros=1, name="pack_panels")(parts, spread)
+    panels = lax.all_to_all(panels, "zl", 0, 0)
+    merged = call(merge_panels, shape((NB + SUB, TILE), bf16), [VMEM], micros=1, name="merge_panels")(panels)
+    ring = lax.all_gather(merged, "zh")
+    plane = call(
         spread_back,
-        shape((32, SUB, TILE), bf16),
+        shape((32, TILE, TILE), bf16),
         [VMEM] * 2,
         [pltpu.VMEM((1024, TILE), bf16)],
         name="spread_back",
     )(adjacent, ring)
-    plane = jnp.concatenate([source_terms, jnp.broadcast_to(weight_rows, (32, SUB, TILE))], axis=1)
     plane = lax.all_to_all(plane, PLANE, 0, 0)
     feature_grad, weight_grad = call(
         finish, (shape((SUB, TILE), bf16), shape((512, 512), jnp.float32)), [VMEM] * 2, name="finish"

time: 153 us -> 140 us (0.915)
  blocking collectives: 41 us -> 80.1 us
  starting transfers between devices: 45.3 us -> 19.8 us
  waiting for transfers between devices: 40.4 us -> 17.6 us
  local copies, waits for them, and re-layouts: 8.58 us -> 6.3 us
    all_gather x0 -> x2, blocking collectives: none -> 41.3 us  [the longest x1 24.8 us: local(): ring_piece = lax.all_gather(piece, 'zh')]
    all_to_all x3 -> x1, starting transfers between devices: 25.1 us -> 3.98 us  [local(): parts = lax.all_to_all(terms.reshape(32, 16, 512), PLANE, 0, 0)]
    all_to_all x3 -> x1, waiting for transfers between devices: 23.7 us -> 6.18 us  [local(): parts = lax.all_to_all(terms.reshape(32, 16, 512), PLANE, 0, 0)]
    all_to_all x1, blocking collectives: 15.2 us -> 8.28 us  [local(): panels = lax.all_to_all(panels, 'zl', 0, 0)]
    all_to_all x1, waiting for transfers between devices: 7.78 us -> 2.59 us  [local(): lax.all_to_all(jnp.broadcast_to(ring_piece[:, :SUB], (16, 4, SUB, TILE)),...]
    all_to_all x1, starting transfers between devices: 13.4 us -> 9.11 us  [local(): panels = lax.all_to_all(partial, ('c', 'zl'), 0, 0)]
    all_gather x1, blocking collectives: 2.51 us -> 5.54 us  [local(): codes = lax.all_gather(code, 'c')]
    unnamed x20, local copies, waits for them, and re-layouts: 7.07 us -> 4.9 us
  transfers between devices with their start and end apart: 5 -> 3, of which waited for: 5 -> 3; matrix products, arithmetic and copies ran while one was open for 0% -> 0% of each run, Pallas kernels for 5% -> 5%
where the time goes in v3:
time: 140 us; the launch traced here: 139 us
  blocking collectives  80.1 us (57%)
  starting transfers between devices  19.8 us (14%)
  waiting for transfers between devices  17.6 us (13%)
  Pallas kernels  13.8 us (10%)
  local copies, waits for them, and re-layouts  6.3 us (4%)
  between operations  1.43 us (1%)
    all_to_all x1, blocking collectives, local(): plane = lax.all_to_all(plane, PLANE, 0, 0)  25 us
    all_gather x1, blocking collectives, local(): ring_piece = lax.all_gather(piece, 'zh')  24.8 us
    all_gather x1, blocking collectives, local(): ring = lax.all_gather(merged, 'zh')  16.5 us
    all_to_all x1, starting transfers between devices, local(): panels = lax.all_to_all(partial, ('c', 'zl'), 0, 0)  9.11 us
    all_to_all x1, waiting for transfers between devices, local(): panels = lax.all_to_all(partial, ('c', 'zl'), 0, 0)  8.86 us
    all_to_all x1, blocking collectives, local(): panels = lax.all_to_all(panels, 'zl', 0, 0)  8.28 us
    all_to_all x1, starting transfers between devices, local(): lax.all_to_all(jnp.broadcast_to(ring_piece[:, :SUB], (16, 4, SUB, TILE)),...  6.75 us
    all_to_all x1, waiting for transfers between devices, local(): parts = lax.all_to_all(terms.reshape(32, 16, 512), PLANE, 0, 0)  6.18 us
  transfers between devices with their start and end apart: 3, of which 3 were waited for; matrix products, arithmetic and copies ran while one was open for 0% of the time, Pallas kernels for 5%

profile of v3, /device:TPU:1, one launch (start us, length us, event | category | flops | bytes accessed | tf_op | source)
XLA Modules:
  0.0 139.2 jit_solution(7907062760643867677)
XLA Ops:
  0.6 0.0 copy-start.1
  0.6 0.0 copy-start.3
  1.3 1.6 %prepare.1 = (bf16[208,128]{1,0:T(8,128)(2,1)}, f32[64,1]{1,0:T(8,128)}) custom-call(s32[1]{0:T(128)S(6)} %copy.14.count_ref, bf16[64,128]{1,0:T(8,128)(2,1)} %feature_hbm.1, s32[1,64]{1,0:T(1,128)} %bitcast.21, s32[1,32]{1,0:T(1,128)} %slot_hbm.1, s32[1,32,512]{2,1,0:T(8,128)} %edge_hbm.1), custom_call_target="tpu_custom_call" | custom-call | flops 1000000000 | bytes 1000000 | tf_op jit(solution)/shard_map/prepare/pallas_call | solution.py:267
  3.0 24.8 %all-gather.1 = bf16[832,128]{1,0:T(8,128)(2,1)S(1)} all-gather(bf16[208,128]{1,0:T(8,128)(2,1)} %get-tuple-element.14), channel_id=3, replica_groups=mesh['zh'=4,'x'=4,'y'=4,'c'=2,'zl'=4] {'zh'}, dimensions={0}, use_global_device_ids=true | all-gather | bytes 266240 | tf_op jit(solution)/shard_map/all_gather | solution.py:289
  27.7 1.2 broadcast_in_dim.17
  29.0 6.8 %all-to-all-start = ((bf16[16,4,64,128]{3,2,1,0:T(8,128)(2,1)}), bf16[16,4,64,128]{3,2,1,0:T(8,128)(2,1)S(1)}, u32[]{:S(2)}, u32[]{:S(2)}) async-start(bf16[16,4,64,128]{3,2,1,0:T(8,128)(2,1)} %broadcast_in_dim.17), calls=%async_computation | async-start | bytes 2097152 | tf_op jit(solution)/shard_map/all_to_all | solution.py:293
  35.7 0.0 copy-done.1
  35.7 0.0 copy-done.3
  35.8 0.1 mark_edges.1
  35.8 5.5 %all-gather = s32[80,512]{1,0:T(8,128)S(1)} all-gather(s32[40,512]{1,0:T(8,128)S(1)} %mark_edges.1), channel_id=2, replica_groups=mesh['zh'=4,'x'=4,'y'=4,'c'=2,'zl'=4] {'c'}, dimensions={0}, use_global_device_ids=true | all-gather | bytes 245760 | tf_op jit(solution)/shard_map/all_gather | solution.py:290
  41.4 0.0 copy-start.9
  41.4 2.7 %build_forward.1.wide_ref = bf16[2,256,2048]{2,1,0:T(8,128)(2,1)S(1)} custom-call(s32[2,128]{1,0:T(2,128)S(1)} %bitcast.19, s32[1]{0:T(128)} %bitcast.5.core_ref, s32[2,40,512]{2,1,0:T(8,128)S(1)} %bitcast.18), custom_call_target="tpu_custom_call" | custom-call | flops 6000000000 | bytes 6000000 | tf_op jit(solution)/shard_map/build_forward/pallas_call | solution.py:294
  44.1 0.0 copy-start.6
  44.1 1.3 copy-done.6
  45.4 0.0 copy-start
  45.4 0.0 copy-start.2
  45.4 2.6 %all-to-all-done = bf16[16,4,64,128]{3,2,1,0:T(8,128)(2,1)S(1)} async-done(((bf16[16,4,64,128]{3,2,1,0:T(8,128)(2,1)}), bf16[16,4,64,128]{3,2,1,0:T(8,128)(2,1)S(1)}, u32[]{:S(2)}, u32[]{:S(2)}) %all-to-all-start) | async-done | bytes 1048608 | tf_op jit(solution)/shard_map/all_to_all | solution.py:293
  48.0 0.0 copy-start.7
  48.0 1.6 %copy-done.7 = bf16[2,256,2048]{2,1,0:T(8,128)(2,1)S(1)} copy-done((bf16[2,256,2048]{2,1,0:T(8,128)(2,1)S(1)}, bf16[2,256,2048]{2,1,0:T(8,128)(2,1)}, u32[]{:S(2)}) %copy-start.7) | copy-done | bytes 2097176
  49.6 2.0 %aggregate.1 = f32[8,64,128]{2,1,0:T(8,128)} custom-call(s32[2,128]{1,0:T(2,128)S(1)} %bitcast.20, bf16[2,256,2048]{2,1,0:T(8,128)(2,1)S(1)} %copy-done.7, bf16[4096,128]{1,0:T(8,128)(2,1)S(1)} %bitcast.12), custom_call_target="tpu_custom_call" | custom-call | flops 2000000000 | bytes 2000000 | tf_op jit(solution)/shard_map/aggregate/pallas_call | solution.py:303
  51.6 9.1 %all-to-all-start.1 = ((f32[8,64,128]{2,1,0:T(8,128)}), f32[8,64,128]{2,1,0:T(8,128)S(1)}, u32[]{:S(2)}, u32[]{:S(2)}) async-start(f32[8,64,128]{2,1,0:T(8,128)} %aggregate.1), calls=%async_computation.1 | async-start | bytes 524288 | tf_op jit(solution)/shard_map/all_to_all | solution.py:311
  60.7 0.0 copy-done.9
  60.7 0.1 reshape.20.degree_ref
  60.8 0.1 reshape.22.slot_ref
  60.9 8.9 %all-to-all-done.1.panel_ref = f32[8,64,128]{2,1,0:T(8,128)S(1)} async-done(((f32[8,64,128]{2,1,0:T(8,128)}), f32[8,64,128]{2,1,0:T(8,128)S(1)}, u32[]{:S(2)}, u32[]{:S(2)}) %all-to-all-start.1) | async-done | bytes 262176 | tf_op jit(solution)/shard_map/all_to_all | solution.py:311
  69.8 0.0 copy-done
  69.8 0.0 copy-done.2
  69.8 1.4 %dense.1 = (bf16[64,512]{1,0:T(8,128)(2,1)}, bf16[4,64,128]{2,1,0:T(8,128)(2,1)S(1)}, bf16[512,512]{1,0:T(8,128)(2,1)}) custom-call(s32[1]{0:T(128)} %bitcast.part_ref, f32[8,64,128]{2,1,0:T(8,128)S(1)} %all-to-all-done.1.panel_ref, bf16[512,512]{1,0:T(8,128)(2,1)S(1)} %copy-done, bf16[64,512]{1,0:T(8,128)(2,1)S(1)} %copy-done.2, s32[4,64]{1,0:T(4,128)S(1)} %reshape.20.degree_ref), custom_call_target="tpu_custom_call" | custom-call | flops 2000000000 | bytes 2000000 | tf_op jit(solution)/shard_map/dense/pallas_call | solution.py:312
  71.2 4.0 %all-to-all-start.2 = ((bf16[32,16,512]{2,1,0:T(8,128)(2,1)}), bf16[32,16,512]{2,1,0:T(8,128)(2,1)S(1)}, u32[]{:S(2)}, u32[]{:S(2)}) async-start(bf16[32,16,512]{2,1,0:T(8,128)(2,1)} %bitcast.7), calls=%async_computation.2 | async-start | bytes 1048576 | tf_op jit(solution)/shard_map/all_to_all | solution.py:319
  75.2 3.5 %build_backward.1.adj_ref = bf16[2048,1024]{1,0:T(8,128)(2,1)S(1)} custom-call(s32[128]{0:T(128)S(1)} %reshape.22.slot_ref, s32[1]{0:T(128)} %bitcast.8.quarter_ref, bf16[4,208,128]{2,1,0:T(8,128)(2,1)S(1)} %bitcast.15), custom_call_target="tpu_custom_call" | custom-call | flops 6000000000 | bytes 6000000 | tf_op jit(solution)/shard_map/build_backward/pallas_call | solution.py:320
  78.7 0.0 copy-start.4
  78.7 2.0 %copy-done.4 = bf16[2048,1024]{1,0:T(8,128)(2,1)} copy-done((bf16[2048,1024]{1,0:T(8,128)(2,1)}, bf16[2048,1024]{1,0:T(8,128)(2,1)S(1)}, u32[]{:S(2)}) %copy-start.4) | copy-done | bytes 4194328
  80.7 6.2 %all-to-all-done.2.part_ref = bf16[32,16,512]{2,1,0:T(8,128)(2,1)S(1)} async-done(((bf16[32,16,512]{2,1,0:T(8,128)(2,1)}), bf16[32,16,512]{2,1,0:T(8,128)(2,1)S(1)}, u32[]{:S(2)}, u32[]{:S(2)}) %all-to-all-start.2) | async-done | bytes 524320 | tf_op jit(solution)/shard_map/all_to_all | solution.py:319
  86.8 0.0 copy-start.5
  86.8 0.1 pack_panels.1
  86.9 8.3 %all_to_all.25.panel_ref = bf16[4,128,128]{2,1,0:T(8,128)(2,1)S(1)} all-to-all(bf16[4,128,128]{2,1,0:T(8,128)(2,1)S(1)} %pack_panels.1), channel_id=1, replica_groups=mesh['zh'=4,'x'=4,'y'=4,'c'=2,'zl'=4] {'zl'}, dimensions={0} | all-to-all | bytes 262144 | tf_op jit(solution)/shard_map/all_to_all | solution.py:330
  95.2 16.5 %all-gather.2 = bf16[1280,128]{1,0:T(8,128)(2,1)S(1)} all-gather(bf16[320,128]{1,0:T(8,128)(2,1)S(1)} %merge_panels.1), channel_id=4, replica_groups=mesh['zh'=4,'x'=4,'y'=4,'c'=2,'zl'=4] {'zh'}, dimensions={0}, use_global_device_ids=true | all-gather | bytes 409600 | tf_op jit(solution)/shard_map/all_gather | solution.py:332
  111.7 0.0 copy-done.5
  111.7 0.0 copy-start.8
  111.7 1.3 spread_back.1
  113.0 25.0 %all_to_all.26.plane_ref = bf16[32,128,128]{2,1,0:T(8,128)(2,1)S(1)} all-to-all(bf16[32,128,128]{2,1,0:T(8,128)(2,1)S(1)} %spread_back.1), channel_id=1, replica_groups=mesh['zh'=4,'x'=4,'y'=4,'c'=2,'zl'=4] {'x','y','c'}, dimensions={0} | all-to-all | bytes 2097152 | tf_op jit(solution)/shard_map/all_to_all | solution.py:340
  138.1 0.0 copy-done.8
  138.1 1.1 finish.1
  (4 shorter events, 0.0 us)
Async XLA Ops:
  0.6 35.1 %copy-start.1 = (s32[1,32,512]{2,1,0:T(8,128)S(1)}, s32[1,32,512]{2,1,0:T(8,128)}, u32[]{:S(2)}) copy-start(s32[1,32,512]{2,1,0:T(8,128)} %edge_hbm.1) | copy-start | bytes 196612
  0.6 35.1 %copy-start.3 = (s32[1,32]{1,0:T(1,128)S(1)}, s32[1,32]{1,0:T(1,128)}, u32[]{:S(2)}) copy-start(s32[1,32]{1,0:T(1,128)} %slot_hbm.1) | copy-start | bytes 388
  29.0 19.0 %all-to-all-start = ((bf16[16,4,64,128]{3,2,1,0:T(8,128)(2,1)}), bf16[16,4,64,128]{3,2,1,0:T(8,128)(2,1)S(1)}, u32[]{:S(2)}, u32[]{:S(2)}) async-start(bf16[16,4,64,128]{3,2,1,0:T(8,128)(2,1)} %broadcast_in_dim.17), calls=%async_computation | async-start | bytes 2097152 | tf_op jit(solution)/shard_map/all_to_all | solution.py:293
  41.4 19.3 %copy-start.9 = (s32[256]{0:T(256)S(1)}, s32[256]{0:T(256)}, u32[]{:S(2)}) copy-start(s32[256]{0:T(256)} %param.14) | copy-start | bytes 3076
  44.1 1.3 copy-start.6
  45.4 24.3 %copy-start = (bf16[512,512]{1,0:T(8,128)(2,1)S(1)}, bf16[512,512]{1,0:T(8,128)(2,1)}, u32[]{:S(2)}) copy-start(bf16[512,512]{1,0:T(8,128)(2,1)} %weight_ref.1) | copy-start | bytes 1572868
  45.4 24.3 %copy-start.2 = (bf16[64,512]{1,0:T(8,128)(2,1)S(1)}, bf16[64,512]{1,0:T(8,128)(2,1)}, u32[]{:S(2)}) copy-start(bf16[64,512]{1,0:T(8,128)(2,1)} %cot_ref.1) | copy-start | bytes 196612
  48.0 1.6 %copy-start.7 = (bf16[2,256,2048]{2,1,0:T(8,128)(2,1)S(1)}, bf16[2,256,2048]{2,1,0:T(8,128)(2,1)}, u32[]{:S(2)}) copy-start(bf16[2,256,2048]{2,1,0:T(8,128)(2,1)} %copy-done.6) | copy-start | bytes 6291460
  51.6 18.2 %all-to-all-start.1 = ((f32[8,64,128]{2,1,0:T(8,128)}), f32[8,64,128]{2,1,0:T(8,128)S(1)}, u32[]{:S(2)}, u32[]{:S(2)}) async-start(f32[8,64,128]{2,1,0:T(8,128)} %aggregate.1), calls=%async_computation.1 | async-start | bytes 524288 | tf_op jit(solution)/shard_map/all_to_all | solution.py:311
  71.2 15.6 %all-to-all-start.2 = ((bf16[32,16,512]{2,1,0:T(8,128)(2,1)}), bf16[32,16,512]{2,1,0:T(8,128)(2,1)S(1)}, u32[]{:S(2)}, u32[]{:S(2)}) async-start(bf16[32,16,512]{2,1,0:T(8,128)(2,1)} %bitcast.7), calls=%async_computation.2 | async-start | bytes 1048576 | tf_op jit(solution)/shard_map/all_to_all | solution.py:319
  78.7 2.0 %copy-start.4 = (bf16[2048,1024]{1,0:T(8,128)(2,1)}, bf16[2048,1024]{1,0:T(8,128)(2,1)S(1)}, u32[]{:S(2)}) copy-start(bf16[2048,1024]{1,0:T(8,128)(2,1)S(1)} %build_backward.1.adj_ref) | copy-start | bytes 12582916
  86.8 24.9 %copy-start.5 = (bf16[2048,1024]{1,0:T(8,128)(2,1)S(1)}, bf16[2048,1024]{1,0:T(8,128)(2,1)}, u32[]{:S(2)}) copy-start(bf16[2048,1024]{1,0:T(8,128)(2,1)} %copy-done.4) | copy-start | bytes 12582916
  111.7 26.3 %copy-start.8 = (f32[64,1]{1,0:T(8,128)S(1)}, f32[64,1]{1,0:T(8,128)}, u32[]{:S(2)}) copy-start(f32[64,1]{1,0:T(8,128)} %get-tuple-element.22.scale_ref) | copy-start | bytes 772

commit v4 on v3

--- a/solution.py
+++ b/solution.py
@@ -78,8 +78,8 @@
     return jnp.where(values == 0.0, -1, row * TILE + col)
 
 
-def onehot(index):
-    positions = lax.broadcasted_iota(jnp.int32, (TILE, index.shape[1]), 0)
+def onehot(index, rows=TILE):
+    positions = lax.broadcasted_iota(jnp.int32, (rows, index.shape[1]), 0)
     return jnp.where(positions == index, jnp.float32(1.0), jnp.float32(0.0)).astype(jnp.bfloat16)
 
 
@@ -131,21 +131,21 @@
     code_ref[0:SLOTS, :] = jnp.where(live, edges, -1)
 
 
-def build_forward(slot_ref, core_ref, code_ref, wide_ref):
-    wide_ref[...] = jnp.zeros_like(wide_ref)
+def build_forward(slot_ref, core_ref, code_ref, degree_ref, tiles_ref, scale_ref):
+    scale_ref[...] = degree_scale(degree_ref[...])
+    tiles_ref[...] = jnp.zeros_like(tiles_ref)
     first = core_ref[0] * SUB
     for b in range(2):
 
         def step(group, carry):
-            for k in range(4):
-                j = group * 4 + k
-                code = code_ref[b, pl.ds(j, 1), :]
-                col = (code & (TILE - 1)) - first
-                col = jnp.where(jnp.logical_and(col >= 0, col < SUB), col + (k % 2) * SUB, -1)
-                tile = nt(onehot(code >> 7), onehot(col)).astype(jnp.bfloat16)
-                row_at = pl.multiple_of(((slot_ref[b, j] >> 6) & 1) * TILE, TILE)
-                lane = pl.multiple_of((group * 2 + k // 2) * TILE, TILE)
-                wide_ref[b, pl.ds(row_at, TILE), pl.ds(lane, TILE)] += tile
+            for k in range(2):
+                pair = []
+                for parity in range(2):
+                    code = code_ref[b, pl.ds(group * 4 + k * 2 + parity, 1), :]
+                    row = onehot(code >> 7)
+                    pair.append(nt(row, onehot((code & (TILE - 1)) - first, SUB)))
+                lane = pl.multiple_of((group * 2 + k) * TILE, TILE)
+                tiles_ref[b, :, pl.ds(lane, TILE)] = jnp.concatenate(pair, axis=1).astype(jnp.bfloat16)
             return carry
 
         lax.fori_loop(0, (slot_ref[b, SLOTS] + 3) >> 2, step, 0)
@@ -187,31 +187,56 @@
     lax.fori_loop(0, (found + 3) >> 2, step, 0)
 
 
-def aggregate(slot_ref, wide_ref, source_ref, out_ref, picked):
+def aggregate(slot_ref, core_ref, tiles_ref, source_ref, own_ref, other_ref, picked):
+    core = core_ref[0]
     for b in range(2):
+        picked[b] = jnp.zeros((SLOTS * SUB, 2 * TILE), jnp.bfloat16)
         for j in range(SLOTS):
-            tile = slot_ref[b, j] & 63
+            slot = slot_ref[b, j]
+            tile = slot & 63
             at = pl.multiple_of(((tile & 15) * 4 + (tile >> 4)) * SUB, SUB)
-            picked[b, j * SUB:(j + 1) * SUB, :] = source_ref[pl.ds(at, SUB), :]
-        total = jnp.dot(wide_ref[b], picked[b], preferred_element_type=jnp.float32)
-        for k in range(4):
-            out_ref[b * 4 + k] = total[k * SUB:(k + 1) * SUB, :]
-
-
-def dense(part_ref, panel_ref, weight_ref, cot_ref, degree_ref, act_ref, spread_ref, term_ref):
+            lane = pl.multiple_of(((slot >> 6) & 1) * TILE, TILE)
+            picked[b, j * SUB:(j + 1) * SUB, pl.ds(lane, TILE)] = source_ref[pl.ds(at, SUB), :]
+        total = jnp.dot(tiles_ref[b], picked[b], preferred_element_type=jnp.float32)
+        for group in range(2):
+            part = total[:, group * TILE:(group + 1) * TILE]
+
+            @pl.when(core == b)
+            def _():
+                own_ref[group * TILE:(group + 1) * TILE, :] = part
+
+            @pl.when(core != b)
+            def _():
+                other_ref[group * TILE:(group + 1) * TILE, :] = part
+
+
+def combine(core_ref, own_ref, other_ref, scale_ref, out_ref):
+    total = (own_ref[...] + other_ref[1 - core_ref[0]]) * scale_ref[...]
+    total = total.astype(jnp.bfloat16)
+    for k in range(4):
+        out_ref[k] = total[k * SUB:(k + 1) * SUB, :]
+
+
+def dense(part_ref, panel_ref, weight_ref, cot_ref, degree_ref, act_ref, spread_ref, pair_ref):
     scale = degree_scale(degree_ref[pl.ds(part_ref[0], 1), :])
-    rows = jnp.concatenate(
-        [((panel_ref[p] + panel_ref[p + 4]) * scale).astype(jnp.bfloat16) for p in range(4)], axis=1
-    )
+    rows = jnp.concatenate([panel_ref[p] for p in range(4)], axis=1)
     pre_act = jnp.dot(rows, weight_ref[...], preferred_element_type=jnp.float32)
     output, slope = gelu_parts(pre_act)
     act_ref[...] = output.astype(jnp.bfloat16)
     pre_grad = (cot_ref[...].astype(jnp.float32) * slope).astype(jnp.bfloat16)
+    pair_ref[0:SUB, :] = rows
+    pair_ref[SUB:TILE, :] = pre_grad
     spread = (nt(pre_grad, weight_ref[...]) * scale).astype(jnp.bfloat16)
     for p in range(4):
         spread_ref[p] = spread[:, p * TILE:(p + 1) * TILE]
-    terms = lax.dot_general(rows, pre_grad, (((0,), (0,)), ((), ())), preferred_element_type=jnp.float32)
-    term_ref[...] = terms.astype(jnp.bfloat16)
+
+
+def weight_terms(core_ref, pair_ref, out_ref):
+    half = pl.ds(pl.multiple_of(core_ref[0] * 256, 256), 256)
+    rows = jnp.concatenate([pair_ref[b, 0:SUB, half] for b in range(2)], axis=0)
+    grads = jnp.concatenate([pair_ref[b, SUB:TILE, :] for b in range(2)], axis=0)
+    terms = lax.dot_general(rows, grads, (((0,), (0,)), ((), ())), preferred_element_type=jnp.float32)
+    out_ref[...] = terms.astype(jnp.bfloat16)
 
 
 def sum_first(ref, first=0, last=None):
@@ -254,7 +279,8 @@
     feature_ref[...] = (total * scale_ref[...]).astype(jnp.bfloat16)
     for s in range(32):
         for p in range(4):
-            weight_ref[s * 16:(s + 1) * 16, p * TILE:(p + 1) * TILE] = plane_ref[
+            at = (s % 2) * 256 + (s // 2) * 16
+            weight_ref[at:at + 16, p * TILE:(p + 1) * TILE] = plane_ref[
                 s, SUB + p * 16:SUB + (p + 1) * 16, :
             ].astype(jnp.float32)
 
@@ -291,32 +317,38 @@
     slots = codes[:, SLOTS, :TILE]
 
     plane_sources = lax.all_to_all(jnp.broadcast_to(ring_piece[:, :SUB], (16, 4, SUB, TILE)), ("x", "y"), 0, 0)
-    wide = call(
+    tiles, dst_scale = call(
         build_forward,
-        shape((2, NB, SLOTS * SUB), bf16),
-        [SMEM, SMEM, VMEM],
+        (shape((2, TILE, SLOTS * SUB), bf16), shape((NB, 1), jnp.float32)),
+        [SMEM, SMEM, VMEM, VMEM],
         micros=6,
         name="build_forward",
-    )(slots, core[None], codes)
-    plane_sources, wide = lax.optimization_barrier((plane_sources, wide))
-
-    partial = call(
+    )(slots, core[None], codes, deg_dst[None])
+    plane_sources, tiles = lax.optimization_barrier((plane_sources, tiles))
+
+    own_sum, other_sum = call(
         aggregate,
-        shape((8, SUB, TILE), jnp.float32),
-        [SMEM, VMEM, VMEM],
-        [pltpu.VMEM((2, SLOTS * SUB, TILE), bf16)],
+        (shape((NB, TILE), jnp.float32), shape((NB, TILE), jnp.float32)),
+        [SMEM, SMEM, VMEM, VMEM],
+        [pltpu.VMEM((2, SLOTS * SUB, 2 * TILE), bf16)],
         name="aggregate",
-    )(slots, wide, plane_sources.reshape(64 * SUB, TILE))
-
-    panels = lax.all_to_all(partial, ("c", "zl"), 0, 0)
-    activated, spread, terms = call(
+    )(slots, core[None], tiles, plane_sources.reshape(64 * SUB, TILE))
+    aggregated = call(combine, shape((4, SUB, TILE), bf16), [SMEM, VMEM, VMEM, VMEM], micros=1, name="combine")(
+        core[None], own_sum, lax.all_gather(other_sum, "c"), dst_scale
+    )
+
+    panels = lax.all_to_all(aggregated, "zl", 0, 0)
+    activated, spread, pair = call(
         dense,
-        (shape((SUB, 512), bf16), shape((4, SUB, TILE), bf16), shape((512, 512), bf16)),
+        (shape((SUB, 512), bf16), shape((4, SUB, TILE), bf16), shape((TILE, 512), bf16)),
         [SMEM] + [VMEM] * 4,
         name="dense",
     )(zl[None], panels, weight, cotangent, deg_dst.reshape(4, SUB))
-
-    parts = lax.all_to_all(terms.reshape(32, 16, 512), PLANE, 0, 0)
+    terms = call(weight_terms, shape((256, 512), bf16), [SMEM, VMEM], micros=1, name="weight_terms")(
+        core[None], lax.all_gather(pair, "c")
+    )
+
+    parts = lax.all_to_all(terms.reshape(16, 16, 512), ("x", "y"), 0, 0)
     adjacent = call(
         build_backward,
         shape((2048, 1024), bf16),

time: 140 us -> 138 us (0.986)
  blocking collectives: 80.1 us -> 93.4 us
  waiting for transfers between devices: 17.6 us -> 9.9 us
  starting transfers between devices: 19.8 us -> 13.6 us
  local copies, waits for them, and re-layouts: 6.3 us -> 3.39 us
  Pallas kernels: 13.8 us -> 15.3 us
    all_gather x0 -> x2, blocking collectives: none -> 10.4 us  [the longest x1 7.41 us: local(): lax.all_gather(other_sum, 'c')]
    all_to_all x2, waiting for transfers between devices: 15 us -> 6.09 us  [the longest x1 4.47 us: local(): panels = lax.all_to_all(aggregated, 'zl', 0, 0)]
    all_to_all x2, starting transfers between devices: 13.1 us -> 6.82 us  [the longest x1 3.53 us: local(): parts = lax.all_to_all(terms.reshape(16, 16, 512), ('x', 'y'), 0, 0)]
    unnamed x20 -> x16, local copies, waits for them, and re-layouts: 4.9 us -> 1.99 us
    all_to_all x1, blocking collectives: 25 us -> 27 us  [local(): plane = lax.all_to_all(plane, PLANE, 0, 0)]
    all_gather x1, blocking collectives: 16.5 us -> 18.3 us  [local(): ring = lax.all_gather(merged, 'zh')]
    pallas_call x2 -> x4, Pallas kernels: 4.69 us -> 6.15 us  [the longest x1 2.83 us: local(): call(build_forward, (shape((2, TILE, SLOTS * SUB), bf16), shape((NB, 1),...]
where the time goes in v4:
time: 138 us; the launch traced here: 137 us
  blocking collectives  93.4 us (68%)
  Pallas kernels  15.3 us (11%)
  starting transfers between devices  13.6 us (10%)
  waiting for transfers between devices  9.9 us (7%)
  local copies, waits for them, and re-layouts  3.39 us (2%)
  between operations  1.44 us (1%)
    all_to_all x1, blocking collectives, local(): plane = lax.all_to_all(plane, PLANE, 0, 0)  27 us
    all_gather x1, blocking collectives, local(): ring_piece = lax.all_gather(piece, 'zh')  24.8 us
    all_gather x1, blocking collectives, local(): ring = lax.all_gather(merged, 'zh')  18.3 us
    all_to_all x1, blocking collectives, local(): panels = lax.all_to_all(panels, 'zl', 0, 0)  7.42 us
    all_gather x1, blocking collectives, local(): lax.all_gather(other_sum, 'c')  7.41 us
    all_to_all x1, starting transfers between devices, local(): lax.all_to_all(jnp.broadcast_to(ring_piece[:, :SUB], (16, 4, SUB, TILE)),...  6.75 us
    all_gather x1, blocking collectives, local(): codes = lax.all_gather(code, 'c')  5.54 us
    all_to_all x1, waiting for transfers between devices, local(): panels = lax.all_to_all(aggregated, 'zl', 0, 0)  4.47 us
  transfers between devices with their start and end apart: 3, of which 3 were waited for; matrix products, arithmetic and copies ran while one was open for 0% of the time, Pallas kernels for 5%

profile of v4, /device:TPU:1, one launch (start us, length us, event | category | flops | bytes accessed | tf_op | source)
XLA Modules:
  0.0 137.1 jit_solution(3405307169835146867)
XLA Ops:
  0.6 0.0 copy-start.2
  0.6 0.0 copy-start.4
  1.3 1.6 %prepare.1 = (bf16[208,128]{1,0:T(8,128)(2,1)}, f32[64,1]{1,0:T(8,128)}) custom-call(s32[1]{0:T(128)S(6)} %copy.14.count_ref, bf16[64,128]{1,0:T(8,128)(2,1)} %feature_hbm.1, s32[1,64]{1,0:T(1,128)} %bitcast.27, s32[1,32]{1,0:T(1,128)} %slot_hbm.1, s32[1,32,512]{2,1,0:T(8,128)} %edge_hbm.1), custom_call_target="tpu_custom_call" | custom-call | flops 1000000000 | bytes 1000000 | tf_op jit(solution)/shard_map/prepare/pallas_call | solution.py:293
  3.0 0.0 copy-start
  3.0 24.8 %all-gather.1 = bf16[832,128]{1,0:T(8,128)(2,1)S(1)} all-gather(bf16[208,128]{1,0:T(8,128)(2,1)} %get-tuple-element.18), channel_id=3, replica_groups=mesh['zh'=4,'x'=4,'y'=4,'c'=2,'zl'=4] {'zh'}, dimensions={0}, use_global_device_ids=true | all-gather | bytes 266240 | tf_op jit(solution)/shard_map/all_gather | solution.py:315
  27.8 1.2 broadcast_in_dim.24
  29.0 6.8 %all-to-all-start = ((bf16[16,4,64,128]{3,2,1,0:T(8,128)(2,1)}), bf16[16,4,64,128]{3,2,1,0:T(8,128)(2,1)S(1)}, u32[]{:S(2)}, u32[]{:S(2)}) async-start(bf16[16,4,64,128]{3,2,1,0:T(8,128)(2,1)} %broadcast_in_dim.24), calls=%async_computation | async-start | bytes 2097152 | tf_op jit(solution)/shard_map/all_to_all | solution.py:319
  35.8 0.0 copy-done.2
  35.8 0.0 copy-done.4
  35.8 0.1 mark_edges.1
  35.8 5.5 %all-gather = s32[80,512]{1,0:T(8,128)S(1)} all-gather(s32[40,512]{1,0:T(8,128)S(1)} %mark_edges.1), channel_id=2, replica_groups=mesh['zh'=4,'x'=4,'y'=4,'c'=2,'zl'=4] {'c'}, dimensions={0}, use_global_device_ids=true | all-gather | bytes 245760 | tf_op jit(solution)/shard_map/all_gather | solution.py:316
  41.4 0.0 copy-done
  41.4 2.8 %build_forward.1 = (bf16[2,128,2048]{2,1,0:T(8,128)(2,1)S(1)}, f32[256,1]{1,0:T(8,128)S(1)}) custom-call(s32[2,128]{1,0:T(2,128)S(1)} %bitcast.25, s32[1]{0:T(128)} %bitcast.1.core_ref, s32[2,40,512]{2,1,0:T(8,128)S(1)} %bitcast.23, s32[1,256]{1,0:T(1,128)S(1)} %bitcast.24), custom_call_target="tpu_custom_call" | custom-call | flops 6000000000 | bytes 6000000 | tf_op jit(solution)/shard_map/build_forward/pallas_call | solution.py:320
  44.2 3.8 %all-to-all-done = bf16[16,4,64,128]{3,2,1,0:T(8,128)(2,1)S(1)} async-done(((bf16[16,4,64,128]{3,2,1,0:T(8,128)(2,1)}), bf16[16,4,64,128]{3,2,1,0:T(8,128)(2,1)S(1)}, u32[]{:S(2)}, u32[]{:S(2)}) %all-to-all-start) | async-done | bytes 1048608 | tf_op jit(solution)/shard_map/all_to_all | solution.py:319
  48.0 0.0 copy-start.1
  48.0 0.0 copy-start.3
  48.0 1.6 %aggregate.1 = (f32[256,128]{1,0:T(8,128)S(1)}, f32[256,128]{1,0:T(8,128)S(1)}) custom-call(s32[2,128]{1,0:T(2,128)S(1)} %bitcast.26, s32[1]{0:T(128)} %bitcast.1.core_ref, bf16[2,128,2048]{2,1,0:T(8,128)(2,1)S(1)} %get-tuple-element.20.tiles_ref, bf16[4096,128]{1,0:T(8,128)(2,1)S(1)} %bitcast.15), custom_call_target="tpu_custom_call" | custom-call | flops 2000000000 | bytes 2000000 | tf_op jit(solution)/shard_map/aggregate/pallas_call | solution.py:329
  49.7 7.4 %all-gather.2 = f32[512,128]{1,0:T(8,128)S(1)} all-gather(f32[256,128]{1,0:T(8,128)S(1)} %get-tuple-element.23), channel_id=4, replica_groups=mesh['zh'=4,'x'=4,'y'=4,'c'=2,'zl'=4] {'c'}, dimensions={0}, use_global_device_ids=true | all-gather | bytes 393216 | tf_op jit(solution)/shard_map/all_gather | solution.py:337
  57.1 0.7 combine.1
  57.8 3.3 %all-to-all-start.1 = ((bf16[4,64,128]{2,1,0:T(8,128)(2,1)}), bf16[4,64,128]{2,1,0:T(8,128)(2,1)S(1)}, u32[]{:S(2)}, u32[]{:S(2)}) async-start(bf16[4,64,128]{2,1,0:T(8,128)(2,1)} %combine.1), calls=%async_computation.1 | async-start | bytes 131072 | tf_op jit(solution)/shard_map/all_to_all | solution.py:340
  61.1 0.1 reshape.20.degree_ref
  61.2 0.1 reshape.22.slot_ref
  61.3 4.5 %all-to-all-done.1.panel_ref = bf16[4,64,128]{2,1,0:T(8,128)(2,1)S(1)} async-done(((bf16[4,64,128]{2,1,0:T(8,128)(2,1)}), bf16[4,64,128]{2,1,0:T(8,128)(2,1)S(1)}, u32[]{:S(2)}, u32[]{:S(2)}) %all-to-all-start.1) | async-done | bytes 65568 | tf_op jit(solution)/shard_map/all_to_all | solution.py:340
  65.8 0.0 copy-done.1
  65.8 0.0 copy-done.3
  65.8 0.9 dense.1
  66.7 3.0 %all-gather.3 = bf16[256,512]{1,0:T(8,128)(2,1)S(1)} all-gather(bf16[128,512]{1,0:T(8,128)(2,1)S(1)} %get-tuple-element.26), channel_id=5, replica_groups=mesh['zh'=4,'x'=4,'y'=4,'c'=2,'zl'=4] {'c'}, dimensions={0}, use_global_device_ids=true | all-gather | bytes 393216 | tf_op jit(solution)/shard_map/all_gather | solution.py:348
  69.7 1.0 weight_terms.1
  70.7 3.5 %all-to-all-start.2 = ((bf16[16,16,512]{2,1,0:T(8,128)(2,1)}), bf16[16,16,512]{2,1,0:T(8,128)(2,1)S(1)}, u32[]{:S(2)}, u32[]{:S(2)}) async-start(bf16[16,16,512]{2,1,0:T(8,128)(2,1)} %bitcast.10), calls=%async_computation.2 | async-start | bytes 524288 | tf_op jit(solution)/shard_map/all_to_all | solution.py:351
  74.2 4.1 %build_backward.1.adj_ref = bf16[2048,1024]{1,0:T(8,128)(2,1)S(1)} custom-call(s32[128]{0:T(128)S(1)} %reshape.22.slot_ref, s32[1]{0:T(128)} %bitcast.11.quarter_ref, bf16[4,208,128]{2,1,0:T(8,128)(2,1)S(1)} %bitcast.18), custom_call_target="tpu_custom_call" | custom-call | flops 6000000000 | bytes 6000000 | tf_op jit(solution)/shard_map/build_backward/pallas_call | solution.py:352
  78.4 0.0 copy-start.5
  78.4 2.0 %copy-done.5 = bf16[2048,1024]{1,0:T(8,128)(2,1)} copy-done((bf16[2048,1024]{1,0:T(8,128)(2,1)}, bf16[2048,1024]{1,0:T(8,128)(2,1)S(1)}, u32[]{:S(2)}) %copy-start.5) | copy-done | bytes 4194328
  80.3 1.6 %all-to-all-done.2.part_ref = bf16[16,16,512]{2,1,0:T(8,128)(2,1)S(1)} async-done(((bf16[16,16,512]{2,1,0:T(8,128)(2,1)}), bf16[16,16,512]{2,1,0:T(8,128)(2,1)S(1)}, u32[]{:S(2)}, u32[]{:S(2)}) %all-to-all-start.2) | async-done | bytes 262176 | tf_op jit(solution)/shard_map/all_to_all | solution.py:351
  82.0 0.0 copy-start.6
  82.0 7.4 %all_to_all.25.panel_ref = bf16[4,128,128]{2,1,0:T(8,128)(2,1)S(1)} all-to-all(bf16[4,128,128]{2,1,0:T(8,128)(2,1)S(1)} %pack_panels.1), channel_id=1, replica_groups=mesh['zh'=4,'x'=4,'y'=4,'c'=2,'zl'=4] {'zl'}, dimensions={0} | all-to-all | bytes 262144 | tf_op jit(solution)/shard_map/all_to_all | solution.py:362
  89.4 18.3 %all-gather.4 = bf16[1280,128]{1,0:T(8,128)(2,1)S(1)} all-gather(bf16[320,128]{1,0:T(8,128)(2,1)S(1)} %merge_panels.1), channel_id=6, replica_groups=mesh['zh'=4,'x'=4,'y'=4,'c'=2,'zl'=4] {'zh'}, dimensions={0}, use_global_device_ids=true | all-gather | bytes 409600 | tf_op jit(solution)/shard_map/all_gather | solution.py:364
  107.7 0.0 copy-done.6
  107.7 0.0 copy-start.7
  107.7 1.3 spread_back.1
  109.0 27.0 %all_to_all.26.plane_ref = bf16[32,128,128]{2,1,0:T(8,128)(2,1)S(1)} all-to-all(bf16[32,128,128]{2,1,0:T(8,128)(2,1)S(1)} %spread_back.1), channel_id=1, replica_groups=mesh['zh'=4,'x'=4,'y'=4,'c'=2,'zl'=4] {'x','y','c'}, dimensions={0} | all-to-all | bytes 2097152 | tf_op jit(solution)/shard_map/all_to_all | solution.py:372
  136.0 0.0 copy-done.7
  136.0 1.1 finish.1
  (5 shorter events, 0.1 us)
Async XLA Ops:
  0.6 35.1 %copy-start.2 = (s32[1,32,512]{2,1,0:T(8,128)S(1)}, s32[1,32,512]{2,1,0:T(8,128)}, u32[]{:S(2)}) copy-start(s32[1,32,512]{2,1,0:T(8,128)} %edge_hbm.1) | copy-start | bytes 196612
  0.6 35.1 %copy-start.4 = (s32[1,32]{1,0:T(1,128)S(1)}, s32[1,32]{1,0:T(1,128)}, u32[]{:S(2)}) copy-start(s32[1,32]{1,0:T(1,128)} %slot_hbm.1) | copy-start | bytes 388
  3.0 38.4 %copy-start = (s32[256]{0:T(256)S(1)}, s32[256]{0:T(256)}, u32[]{:S(2)}) copy-start(s32[256]{0:T(256)} %param.14) | copy-start | bytes 3076
  29.0 19.0 %all-to-all-start = ((bf16[16,4,64,128]{3,2,1,0:T(8,128)(2,1)}), bf16[16,4,64,128]{3,2,1,0:T(8,128)(2,1)S(1)}, u32[]{:S(2)}, u32[]{:S(2)}) async-start(bf16[16,4,64,128]{3,2,1,0:T(8,128)(2,1)} %broadcast_in_dim.24), calls=%async_computation | async-start | bytes 2097152 | tf_op jit(solution)/shard_map/all_to_all | solution.py:319
  48.0 17.7 %copy-start.1 = (bf16[512,512]{1,0:T(8,128)(2,1)S(1)}, bf16[512,512]{1,0:T(8,128)(2,1)}, u32[]{:S(2)}) copy-start(bf16[512,512]{1,0:T(8,128)(2,1)} %weight_ref.1) | copy-start | bytes 1572868
  48.0 17.8 %copy-start.3 = (bf16[64,512]{1,0:T(8,128)(2,1)S(1)}, bf16[64,512]{1,0:T(8,128)(2,1)}, u32[]{:S(2)}) copy-start(bf16[64,512]{1,0:T(8,128)(2,1)} %cot_ref.1) | copy-start | bytes 196612
  57.8 8.0 %all-to-all-start.1 = ((bf16[4,64,128]{2,1,0:T(8,128)(2,1)}), bf16[4,64,128]{2,1,0:T(8,128)(2,1)S(1)}, u32[]{:S(2)}, u32[]{:S(2)}) async-start(bf16[4,64,128]{2,1,0:T(8,128)(2,1)} %combine.1), calls=%async_computation.1 | async-start | bytes 131072 | tf_op jit(solution)/shard_map/all_to_all | solution.py:340
  70.7 11.3 %all-to-all-start.2 = ((bf16[16,16,512]{2,1,0:T(8,128)(2,1)}), bf16[16,16,512]{2,1,0:T(8,128)(2,1)S(1)}, u32[]{:S(2)}, u32[]{:S(2)}) async-start(bf16[16,16,512]{2,1,0:T(8,128)(2,1)} %bitcast.10), calls=%async_computation.2 | async-start | bytes 524288 | tf_op jit(solution)/shard_map/all_to_all | solution.py:351
  78.4 2.0 %copy-start.5 = (bf16[2048,1024]{1,0:T(8,128)(2,1)}, bf16[2048,1024]{1,0:T(8,128)(2,1)S(1)}, u32[]{:S(2)}) copy-start(bf16[2048,1024]{1,0:T(8,128)(2,1)S(1)} %build_backward.1.adj_ref) | copy-start | bytes 12582916
  82.0 25.8 %copy-start.6 = (bf16[2048,1024]{1,0:T(8,128)(2,1)S(1)}, bf16[2048,1024]{1,0:T(8,128)(2,1)}, u32[]{:S(2)}) copy-start(bf16[2048,1024]{1,0:T(8,128)(2,1)} %copy-done.5) | copy-start | bytes 12582916
  107.7 28.2 %copy-start.7 = (f32[64,1]{1,0:T(8,128)S(1)}, f32[64,1]{1,0:T(8,128)}, u32[]{:S(2)}) copy-start(f32[64,1]{1,0:T(8,128)} %get-tuple-element.30.scale_ref) | copy-start | bytes 772

commit v5 on v4

--- a/solution.py
+++ b/solution.py
@@ -217,26 +217,18 @@
         out_ref[k] = total[k * SUB:(k + 1) * SUB, :]
 
 
-def dense(part_ref, panel_ref, weight_ref, cot_ref, degree_ref, act_ref, spread_ref, pair_ref):
+def dense(part_ref, panel_ref, weight_ref, cot_ref, degree_ref, act_ref, spread_ref, term_ref):
     scale = degree_scale(degree_ref[pl.ds(part_ref[0], 1), :])
     rows = jnp.concatenate([panel_ref[p] for p in range(4)], axis=1)
     pre_act = jnp.dot(rows, weight_ref[...], preferred_element_type=jnp.float32)
     output, slope = gelu_parts(pre_act)
     act_ref[...] = output.astype(jnp.bfloat16)
     pre_grad = (cot_ref[...].astype(jnp.float32) * slope).astype(jnp.bfloat16)
-    pair_ref[0:SUB, :] = rows
-    pair_ref[SUB:TILE, :] = pre_grad
     spread = (nt(pre_grad, weight_ref[...]) * scale).astype(jnp.bfloat16)
     for p in range(4):
         spread_ref[p] = spread[:, p * TILE:(p + 1) * TILE]
-
-
-def weight_terms(core_ref, pair_ref, out_ref):
-    half = pl.ds(pl.multiple_of(core_ref[0] * 256, 256), 256)
-    rows = jnp.concatenate([pair_ref[b, 0:SUB, half] for b in range(2)], axis=0)
-    grads = jnp.concatenate([pair_ref[b, SUB:TILE, :] for b in range(2)], axis=0)
-    terms = lax.dot_general(rows, grads, (((0,), (0,)), ((), ())), preferred_element_type=jnp.float32)
-    out_ref[...] = terms.astype(jnp.bfloat16)
+    terms = lax.dot_general(rows, pre_grad, (((0,), (0,)), ((), ())), preferred_element_type=jnp.float32)
+    term_ref[...] = terms.astype(jnp.bfloat16)
 
 
 def sum_first(ref, first=0, last=None):
@@ -279,8 +271,7 @@
     feature_ref[...] = (total * scale_ref[...]).astype(jnp.bfloat16)
     for s in range(32):
         for p in range(4):
-            at = (s % 2) * 256 + (s // 2) * 16
-            weight_ref[at:at + 16, p * TILE:(p + 1) * TILE] = plane_ref[
+            weight_ref[s * 16:(s + 1) * 16, p * TILE:(p + 1) * TILE] = plane_ref[
                 s, SUB + p * 16:SUB + (p + 1) * 16, :
             ].astype(jnp.float32)
 
@@ -338,17 +329,14 @@
     )
 
     panels = lax.all_to_all(aggregated, "zl", 0, 0)
-    activated, spread, pair = call(
+    activated, spread, terms = call(
         dense,
-        (shape((SUB, 512), bf16), shape((4, SUB, TILE), bf16), shape((TILE, 512), bf16)),
+        (shape((SUB, 512), bf16), shape((4, SUB, TILE), bf16), shape((512, 512), bf16)),
         [SMEM] + [VMEM] * 4,
         name="dense",
     )(zl[None], panels, weight, cotangent, deg_dst.reshape(4, SUB))
-    terms = call(weight_terms, shape((256, 512), bf16), [SMEM, VMEM], micros=1, name="weight_terms")(
-        core[None], lax.all_gather(pair, "c")
-    )
-
-    parts = lax.all_to_all(terms.reshape(16, 16, 512), ("x", "y"), 0, 0)
+
+    parts = lax.all_to_all(terms.reshape(32, 16, 512), PLANE, 0, 0)
     adjacent = call(
         build_backward,
         shape((2048, 1024), bf16),

time: 138 us -> 137 us (level)
  blocking collectives: 93.4 us -> 87.5 us
  waiting for transfers between devices: 9.9 us -> 13.1 us
  starting transfers between devices: 13.6 us -> 15.1 us
    all_to_all x1, waiting for transfers between devices: 1.62 us -> 5.2 us  [local(): parts = lax.all_to_all(terms.reshape(32, 16, 512), PLANE, 0, 0)]
    all_gather x1 -> x0, blocking collectives: 3.03 us -> none  [local(): lax.all_gather(pair, 'c')]
    all_to_all x1, blocking collectives: 27 us -> 25 us  [local(): plane = lax.all_to_all(plane, PLANE, 0, 0)]
    all_gather x1, blocking collectives: 18.3 us -> 16.5 us  [local(): ring = lax.all_gather(merged, 'zh')]
    all_to_all x1, starting transfers between devices: 3.53 us -> 5.04 us  [local(): parts = lax.all_to_all(terms.reshape(32, 16, 512), PLANE, 0, 0)]
  transfers between devices with their start and end apart: 3 -> 3, of which waited for: 3 -> 3; matrix products, arithmetic and copies ran while one was open for 0% -> 0% of each run, Pallas kernels for 5% -> 6%
where the time goes in v5:
time: 137 us; the launch traced here: 136 us
  blocking collectives  87.5 us (64%)
  Pallas kernels  15.6 us (11%)
  starting transfers between devices  15.1 us (11%)
  waiting for transfers between devices  13.1 us (10%)
  local copies, waits for them, and re-layouts  3.39 us (2%)
  between operations  1.44 us (1%)
    all_to_all x1, blocking collectives, local(): plane = lax.all_to_all(plane, PLANE, 0, 0)  25 us
    all_gather x1, blocking collectives, local(): ring_piece = lax.all_gather(piece, 'zh')  24.8 us
    all_gather x1, blocking collectives, local(): ring = lax.all_gather(merged, 'zh')  16.5 us
    all_to_all x1, blocking collectives, local(): panels = lax.all_to_all(panels, 'zl', 0, 0)  8.28 us
    all_gather x1, blocking collectives, local(): lax.all_gather(other_sum, 'c')  7.41 us
    all_to_all x1, starting transfers between devices, local(): lax.all_to_all(jnp.broadcast_to(ring_piece[:, :SUB], (16, 4, SUB, TILE)),...  6.75 us
    all_gather x1, blocking collectives, local(): codes = lax.all_gather(code, 'c')  5.54 us
    all_to_all x1, waiting for transfers between devices, local(): parts = lax.all_to_all(terms.reshape(32, 16, 512), PLANE, 0, 0)  5.2 us
  transfers between devices with their start and end apart: 3, of which 3 were waited for; matrix products, arithmetic and copies ran while one was open for 0% of the time, Pallas kernels for 6%

profile of v5, /device:TPU:1, one launch (start us, length us, event | category | flops | bytes accessed | tf_op | source)
XLA Modules:
  0.0 136.2 jit_solution(12150928805003970543)
XLA Ops:
  0.6 0.0 copy-start.2
  0.6 0.0 copy-start.4
  1.3 1.6 %prepare.1 = (bf16[208,128]{1,0:T(8,128)(2,1)}, f32[64,1]{1,0:T(8,128)}) custom-call(s32[1]{0:T(128)S(6)} %copy.14.count_ref, bf16[64,128]{1,0:T(8,128)(2,1)} %feature_hbm.1, s32[1,64]{1,0:T(1,128)} %bitcast.25, s32[1,32]{1,0:T(1,128)} %slot_hbm.1, s32[1,32,512]{2,1,0:T(8,128)} %edge_hbm.1), custom_call_target="tpu_custom_call" | custom-call | flops 1000000000 | bytes 1000000 | tf_op jit(solution)/shard_map/prepare/pallas_call | solution.py:284
  3.0 0.0 copy-start
  3.0 24.8 %all-gather.1 = bf16[832,128]{1,0:T(8,128)(2,1)S(1)} all-gather(bf16[208,128]{1,0:T(8,128)(2,1)} %get-tuple-element.18), channel_id=3, replica_groups=mesh['zh'=4,'x'=4,'y'=4,'c'=2,'zl'=4] {'zh'}, dimensions={0}, use_global_device_ids=true | all-gather | bytes 266240 | tf_op jit(solution)/shard_map/all_gather | solution.py:306
  27.8 1.2 broadcast_in_dim.23
  29.0 6.8 %all-to-all-start = ((bf16[16,4,64,128]{3,2,1,0:T(8,128)(2,1)}), bf16[16,4,64,128]{3,2,1,0:T(8,128)(2,1)S(1)}, u32[]{:S(2)}, u32[]{:S(2)}) async-start(bf16[16,4,64,128]{3,2,1,0:T(8,128)(2,1)} %broadcast_in_dim.23), calls=%async_computation | async-start | bytes 2097152 | tf_op jit(solution)/shard_map/all_to_all | solution.py:310
  35.8 0.0 copy-done.2
  35.8 0.0 copy-done.4
  35.8 0.1 mark_edges.1
  35.8 5.5 %all-gather = s32[80,512]{1,0:T(8,128)S(1)} all-gather(s32[40,512]{1,0:T(8,128)S(1)} %mark_edges.1), channel_id=2, replica_groups=mesh['zh'=4,'x'=4,'y'=4,'c'=2,'zl'=4] {'c'}, dimensions={0}, use_global_device_ids=true | all-gather | bytes 245760 | tf_op jit(solution)/shard_map/all_gather | solution.py:307
  41.4 0.0 copy-done
  41.4 3.2 %build_forward.1 = (bf16[2,128,2048]{2,1,0:T(8,128)(2,1)S(1)}, f32[256,1]{1,0:T(8,128)S(1)}) custom-call(s32[2,128]{1,0:T(2,128)S(1)} %bitcast.23, s32[1]{0:T(128)} %bitcast.1.core_ref, s32[2,40,512]{2,1,0:T(8,128)S(1)} %bitcast.21, s32[1,256]{1,0:T(1,128)S(1)} %bitcast.22), custom_call_target="tpu_custom_call" | custom-call | flops 6000000000 | bytes 6000000 | tf_op jit(solution)/shard_map/build_forward/pallas_call | solution.py:311
  44.6 3.4 %all-to-all-done = bf16[16,4,64,128]{3,2,1,0:T(8,128)(2,1)S(1)} async-done(((bf16[16,4,64,128]{3,2,1,0:T(8,128)(2,1)}), bf16[16,4,64,128]{3,2,1,0:T(8,128)(2,1)S(1)}, u32[]{:S(2)}, u32[]{:S(2)}) %all-to-all-start) | async-done | bytes 1048608 | tf_op jit(solution)/shard_map/all_to_all | solution.py:310
  48.0 0.0 copy-start.1
  48.0 0.0 copy-start.3
  48.0 1.6 %aggregate.1 = (f32[256,128]{1,0:T(8,128)S(1)}, f32[256,128]{1,0:T(8,128)S(1)}) custom-call(s32[2,128]{1,0:T(2,128)S(1)} %bitcast.24, s32[1]{0:T(128)} %bitcast.1.core_ref, bf16[2,128,2048]{2,1,0:T(8,128)(2,1)S(1)} %get-tuple-element.20.tiles_ref, bf16[4096,128]{1,0:T(8,128)(2,1)S(1)} %bitcast.14), custom_call_target="tpu_custom_call" | custom-call | flops 2000000000 | bytes 2000000 | tf_op jit(solution)/shard_map/aggregate/pallas_call | solution.py:320
  49.7 7.4 %all-gather.2 = f32[512,128]{1,0:T(8,128)S(1)} all-gather(f32[256,128]{1,0:T(8,128)S(1)} %get-tuple-element.23), channel_id=4, replica_groups=mesh['zh'=4,'x'=4,'y'=4,'c'=2,'zl'=4] {'c'}, dimensions={0}, use_global_device_ids=true | all-gather | bytes 393216 | tf_op jit(solution)/shard_map/all_gather | solution.py:328
  57.1 0.7 combine.1
  57.8 3.3 %all-to-all-start.1 = ((bf16[4,64,128]{2,1,0:T(8,128)(2,1)}), bf16[4,64,128]{2,1,0:T(8,128)(2,1)S(1)}, u32[]{:S(2)}, u32[]{:S(2)}) async-start(bf16[4,64,128]{2,1,0:T(8,128)(2,1)} %combine.1), calls=%async_computation.1 | async-start | bytes 131072 | tf_op jit(solution)/shard_map/all_to_all | solution.py:331
  61.1 0.1 reshape.20.degree_ref
  61.2 0.1 reshape.22.slot_ref
  61.3 4.5 %all-to-all-done.1.panel_ref = bf16[4,64,128]{2,1,0:T(8,128)(2,1)S(1)} async-done(((bf16[4,64,128]{2,1,0:T(8,128)(2,1)}), bf16[4,64,128]{2,1,0:T(8,128)(2,1)S(1)}, u32[]{:S(2)}, u32[]{:S(2)}) %all-to-all-start.1) | async-done | bytes 65568 | tf_op jit(solution)/shard_map/all_to_all | solution.py:331
  65.8 0.0 copy-done.1
  65.8 0.0 copy-done.3
  65.8 1.4 %dense.1 = (bf16[64,512]{1,0:T(8,128)(2,1)}, bf16[4,64,128]{2,1,0:T(8,128)(2,1)S(1)}, bf16[512,512]{1,0:T(8,128)(2,1)}) custom-call(s32[1]{0:T(128)} %bitcast.part_ref, bf16[4,64,128]{2,1,0:T(8,128)(2,1)S(1)} %all-to-all-done.1.panel_ref, bf16[512,512]{1,0:T(8,128)(2,1)S(1)} %copy-done.1, bf16[64,512]{1,0:T(8,128)(2,1)S(1)} %copy-done.3, ...), custom_call_target="tpu_custom_call" | custom-call | flops 2000000000 | bytes 2000000 | tf_op jit(solution)/shard_map/dense/pallas_call | solution.py:332
  67.2 5.0 %all-to-all-start.2 = ((bf16[32,16,512]{2,1,0:T(8,128)(2,1)}), bf16[32,16,512]{2,1,0:T(8,128)(2,1)S(1)}, u32[]{:S(2)}, u32[]{:S(2)}) async-start(bf16[32,16,512]{2,1,0:T(8,128)(2,1)} %bitcast.9), calls=%async_computation.2 | async-start | bytes 1048576 | tf_op jit(solution)/shard_map/all_to_all | solution.py:339
  72.2 4.5 %build_backward.1.adj_ref = bf16[2048,1024]{1,0:T(8,128)(2,1)S(1)} custom-call(s32[128]{0:T(128)S(1)} %reshape.22.slot_ref, s32[1]{0:T(128)} %bitcast.10.quarter_ref, bf16[4,208,128]{2,1,0:T(8,128)(2,1)S(1)} %bitcast.17), custom_call_target="tpu_custom_call" | custom-call | flops 6000000000 | bytes 6000000 | tf_op jit(solution)/shard_map/build_backward/pallas_call | solution.py:340
  76.7 0.0 copy-start.5
  76.7 2.0 %copy-done.5 = bf16[2048,1024]{1,0:T(8,128)(2,1)} copy-done((bf16[2048,1024]{1,0:T(8,128)(2,1)}, bf16[2048,1024]{1,0:T(8,128)(2,1)S(1)}, u32[]{:S(2)}) %copy-start.5) | copy-done | bytes 4194328
  78.7 5.2 %all-to-all-done.2.part_ref = bf16[32,16,512]{2,1,0:T(8,128)(2,1)S(1)} async-done(((bf16[32,16,512]{2,1,0:T(8,128)(2,1)}), bf16[32,16,512]{2,1,0:T(8,128)(2,1)S(1)}, u32[]{:S(2)}, u32[]{:S(2)}) %all-to-all-start.2) | async-done | bytes 524320 | tf_op jit(solution)/shard_map/all_to_all | solution.py:339
  83.9 0.0 copy-start.6
  83.9 0.1 pack_panels.1
  84.0 8.3 %all_to_all.25.panel_ref = bf16[4,128,128]{2,1,0:T(8,128)(2,1)S(1)} all-to-all(bf16[4,128,128]{2,1,0:T(8,128)(2,1)S(1)} %pack_panels.1), channel_id=1, replica_groups=mesh['zh'=4,'x'=4,'y'=4,'c'=2,'zl'=4] {'zl'}, dimensions={0} | all-to-all | bytes 262144 | tf_op jit(solution)/shard_map/all_to_all | solution.py:350
  92.3 16.5 %all-gather.3 = bf16[1280,128]{1,0:T(8,128)(2,1)S(1)} all-gather(bf16[320,128]{1,0:T(8,128)(2,1)S(1)} %merge_panels.1), channel_id=5, replica_groups=mesh['zh'=4,'x'=4,'y'=4,'c'=2,'zl'=4] {'zh'}, dimensions={0}, use_global_device_ids=true | all-gather | bytes 409600 | tf_op jit(solution)/shard_map/all_gather | solution.py:352
  108.8 0.0 copy-done.6
  108.8 0.0 copy-start.7
  108.8 1.3 spread_back.1
  110.1 25.0 %all_to_all.26.plane_ref = bf16[32,128,128]{2,1,0:T(8,128)(2,1)S(1)} all-to-all(bf16[32,128,128]{2,1,0:T(8,128)(2,1)S(1)} %spread_back.1), channel_id=1, replica_groups=mesh['zh'=4,'x'=4,'y'=4,'c'=2,'zl'=4] {'x','y','c'}, dimensions={0} | all-to-all | bytes 2097152 | tf_op jit(solution)/shard_map/all_to_all | solution.py:360
  135.1 0.0 copy-done.7
  135.1 1.1 finish.1
  (4 shorter events, 0.0 us)
Async XLA Ops:
  0.6 35.1 %copy-start.2 = (s32[1,32,512]{2,1,0:T(8,128)S(1)}, s32[1,32,512]{2,1,0:T(8,128)}, u32[]{:S(2)}) copy-start(s32[1,32,512]{2,1,0:T(8,128)} %edge_hbm.1) | copy-start | bytes 196612
  0.6 35.1 %copy-start.4 = (s32[1,32]{1,0:T(1,128)S(1)}, s32[1,32]{1,0:T(1,128)}, u32[]{:S(2)}) copy-start(s32[1,32]{1,0:T(1,128)} %slot_hbm.1) | copy-start | bytes 388
  3.0 38.4 %copy-start = (s32[256]{0:T(256)S(1)}, s32[256]{0:T(256)}, u32[]{:S(2)}) copy-start(s32[256]{0:T(256)} %param.14) | copy-start | bytes 3076
  29.0 19.0 %all-to-all-start = ((bf16[16,4,64,128]{3,2,1,0:T(8,128)(2,1)}), bf16[16,4,64,128]{3,2,1,0:T(8,128)(2,1)S(1)}, u32[]{:S(2)}, u32[]{:S(2)}) async-start(bf16[16,4,64,128]{3,2,1,0:T(8,128)(2,1)} %broadcast_in_dim.23), calls=%async_computation | async-start | bytes 2097152 | tf_op jit(solution)/shard_map/all_to_all | solution.py:310
  48.0 17.7 %copy-start.1 = (bf16[512,512]{1,0:T(8,128)(2,1)S(1)}, bf16[512,512]{1,0:T(8,128)(2,1)}, u32[]{:S(2)}) copy-start(bf16[512,512]{1,0:T(8,128)(2,1)} %weight_ref.1) | copy-start | bytes 1572868
  48.0 17.8 %copy-start.3 = (bf16[64,512]{1,0:T(8,128)(2,1)S(1)}, bf16[64,512]{1,0:T(8,128)(2,1)}, u32[]{:S(2)}) copy-start(bf16[64,512]{1,0:T(8,128)(2,1)} %cot_ref.1) | copy-start | bytes 196612
  57.8 8.0 %all-to-all-start.1 = ((bf16[4,64,128]{2,1,0:T(8,128)(2,1)}), bf16[4,64,128]{2,1,0:T(8,128)(2,1)S(1)}, u32[]{:S(2)}, u32[]{:S(2)}) async-start(bf16[4,64,128]{2,1,0:T(8,128)(2,1)} %combine.1), calls=%async_computation.1 | async-start | bytes 131072 | tf_op jit(solution)/shard_map/all_to_all | solution.py:331
  67.2 16.7 %all-to-all-start.2 = ((bf16[32,16,512]{2,1,0:T(8,128)(2,1)}), bf16[32,16,512]{2,1,0:T(8,128)(2,1)S(1)}, u32[]{:S(2)}, u32[]{:S(2)}) async-start(bf16[32,16,512]{2,1,0:T(8,128)(2,1)} %bitcast.9), calls=%async_computation.2 | async-start | bytes 1048576 | tf_op jit(solution)/shard_map/all_to_all | solution.py:339
  76.7 2.0 %copy-start.5 = (bf16[2048,1024]{1,0:T(8,128)(2,1)}, bf16[2048,1024]{1,0:T(8,128)(2,1)S(1)}, u32[]{:S(2)}) copy-start(bf16[2048,1024]{1,0:T(8,128)(2,1)S(1)} %build_backward.1.adj_ref) | copy-start | bytes 12582916
  83.9 24.9 %copy-start.6 = (bf16[2048,1024]{1,0:T(8,128)(2,1)S(1)}, bf16[2048,1024]{1,0:T(8,128)(2,1)}, u32[]{:S(2)}) copy-start(bf16[2048,1024]{1,0:T(8,128)(2,1)} %copy-done.5) | copy-start | bytes 12582916
  108.8 26.3 %copy-start.7 = (f32[64,1]{1,0:T(8,128)S(1)}, f32[64,1]{1,0:T(8,128)}, u32[]{:S(2)}) copy-start(f32[64,1]{1,0:T(8,128)} %get-tuple-element.30.scale_ref) | copy-start | bytes 772

commit v6 on v5

--- a/solution.py
+++ b/solution.py
@@ -122,6 +122,12 @@
     out_ref[192:208, :] = slots
 
 
+def fan_out(ring_ref, out_hbm, sems):
+    copies = start_copies(sems, *((ring_ref.at[:, 0:SUB], out_hbm.at[i]) for i in range(16)))
+    for copy in copies:
+        copy.wait()
+
+
 def mark_edges(count_ref, slot_ref, edge_ref, code_ref):
     count = count_ref[0]
     row = jnp.broadcast_to(slot_row(count, slot_ref[...]), (8, TILE))
@@ -190,13 +196,14 @@
 def aggregate(slot_ref, core_ref, tiles_ref, source_ref, own_ref, other_ref, picked):
     core = core_ref[0]
     for b in range(2):
-        picked[b] = jnp.zeros((SLOTS * SUB, 2 * TILE), jnp.bfloat16)
         for j in range(SLOTS):
             slot = slot_ref[b, j]
             tile = slot & 63
             at = pl.multiple_of(((tile & 15) * 4 + (tile >> 4)) * SUB, SUB)
-            lane = pl.multiple_of(((slot >> 6) & 1) * TILE, TILE)
-            picked[b, j * SUB:(j + 1) * SUB, pl.ds(lane, TILE)] = source_ref[pl.ds(at, SUB), :]
+            rows = source_ref[pl.ds(at, SUB), :]
+            first = ((slot >> 6) & 1) == 0
+            picked[b, j * SUB:(j + 1) * SUB, 0:TILE] = jnp.where(first, rows, jnp.zeros_like(rows))
+            picked[b, j * SUB:(j + 1) * SUB, TILE:2 * TILE] = jnp.where(first, jnp.zeros_like(rows), rows)
         total = jnp.dot(tiles_ref[b], picked[b], preferred_element_type=jnp.float32)
         for group in range(2):
             part = total[:, group * TILE:(group + 1) * TILE]
@@ -307,7 +314,16 @@
     codes = lax.all_gather(code, "c")
     slots = codes[:, SLOTS, :TILE]
 
-    plane_sources = lax.all_to_all(jnp.broadcast_to(ring_piece[:, :SUB], (16, 4, SUB, TILE)), ("x", "y"), 0, 0)
+    copies = call(
+        fan_out,
+        shape((16, 4, SUB, TILE), bf16),
+        [VMEM],
+        [pltpu.SemaphoreType.DMA((16,))],
+        micros=1,
+        name="fan_out",
+        out_spec=HBM,
+    )(ring_piece)
+    plane_sources = lax.all_to_all(copies, ("x", "y"), 0, 0)
     tiles, dst_scale = call(
         build_forward,
         (shape((2, TILE, SLOTS * SUB), bf16), shape((NB, 1), jnp.float32)),

time: 137 us -> 136 us (level)
  Pallas kernels: 15.6 us -> 18.1 us
  waiting for transfers between devices: 13.1 us -> 11.7 us
    all_to_all x1, waiting for transfers between devices: 3.45 us -> 1.98 us  [local(): plane_sources = lax.all_to_all(copies, ('x', 'y'), 0, 0)]
    pallas_call x1, Pallas kernels: 3.19 us -> 4.64 us  [local(): call(build_forward, (shape((2, TILE, SLOTS * SUB), bf16), shape((NB, 1),...]
  transfers between devices with their start and end apart: 3 -> 3, of which waited for: 3 -> 3; matrix products, arithmetic and copies ran while one was open for 0% -> 0% of each run, Pallas kernels for 6% -> 7%
where the time goes in v6:
time: 136 us
  blocking collectives  87.6 us (64%)
  Pallas kernels  18.1 us (13%)
  starting transfers between devices  15.1 us (11%)
  waiting for transfers between devices  11.7 us (9%)
  local copies, waits for them, and re-layouts  2.16 us (2%)
  between operations  1.41 us (1%)
    all_to_all x1, blocking collectives, local(): plane = lax.all_to_all(plane, PLANE, 0, 0)  25 us
    all_gather x1, blocking collectives, local(): ring_piece = lax.all_gather(piece, 'zh')  24.8 us
    all_gather x1, blocking collectives, local(): ring = lax.all_gather(merged, 'zh')  16.5 us
    all_to_all x1, blocking collectives, local(): panels = lax.all_to_all(panels, 'zl', 0, 0)  8.28 us
    all_gather x1, blocking collectives, local(): lax.all_gather(other_sum, 'c')  7.41 us
    all_to_all x1, starting transfers between devices, local(): plane_sources = lax.all_to_all(copies, ('x', 'y'), 0, 0)  6.77 us
    all_gather x1, blocking collectives, local(): codes = lax.all_gather(code, 'c')  5.54 us
    all_to_all x1, waiting for transfers between devices, local(): parts = lax.all_to_all(terms.reshape(32, 16, 512), PLANE, 0, 0)  5.23 us
  transfers between devices with their start and end apart: 3, of which 3 were waited for; matrix products, arithmetic and copies ran while one was open for 0% of the time, Pallas kernels for 7%

profile of v6, /device:TPU:1, one launch (start us, length us, event | category | flops | bytes accessed | tf_op | source)
XLA Modules:
  0.0 136.0 jit_solution(4968236456979933380)
XLA Ops:
  1.3 0.0 copy-start.2
  1.3 0.0 copy-start.4
  1.3 1.7 %prepare.1 = (bf16[208,128]{1,0:T(8,128)(2,1)}, f32[64,1]{1,0:T(8,128)}) custom-call(s32[1]{0:T(128)S(6)} %copy.14.count_ref, bf16[64,128]{1,0:T(8,128)(2,1)} %feature_hbm.1, s32[1,64]{1,0:T(1,128)} %bitcast.25, s32[1,32]{1,0:T(1,128)} %slot_hbm.1, s32[1,32,512]{2,1,0:T(8,128)} %edge_hbm.1), custom_call_target="tpu_custom_call" | custom-call | flops 1000000000 | bytes 1000000 | tf_op jit(solution)/shard_map/prepare/pallas_call | solution.py:291
  3.0 24.8 %all-gather.1 = bf16[832,128]{1,0:T(8,128)(2,1)S(1)} all-gather(bf16[208,128]{1,0:T(8,128)(2,1)} %get-tuple-element.18), channel_id=3, replica_groups=mesh['zh'=4,'x'=4,'y'=4,'c'=2,'zl'=4] {'zh'}, dimensions={0}, use_global_device_ids=true | all-gather | bytes 266240 | tf_op jit(solution)/shard_map/all_gather | solution.py:313
  27.7 0.0 copy-start
  27.7 1.1 fan_out.1
  28.8 6.8 %all-to-all-start = ((bf16[16,4,64,128]{3,2,1,0:T(8,128)(2,1)}), bf16[16,4,64,128]{3,2,1,0:T(8,128)(2,1)S(1)}, u32[]{:S(2)}, u32[]{:S(2)}) async-start(bf16[16,4,64,128]{3,2,1,0:T(8,128)(2,1)} %fan_out.1), calls=%async_computation | async-start | bytes 2097152 | tf_op jit(solution)/shard_map/all_to_all | solution.py:326
  35.6 0.0 copy-done.2
  35.6 0.0 copy-done.4
  35.6 0.1 mark_edges.1
  35.7 5.5 %all-gather = s32[80,512]{1,0:T(8,128)S(1)} all-gather(s32[40,512]{1,0:T(8,128)S(1)} %mark_edges.1), channel_id=2, replica_groups=mesh['zh'=4,'x'=4,'y'=4,'c'=2,'zl'=4] {'c'}, dimensions={0}, use_global_device_ids=true | all-gather | bytes 245760 | tf_op jit(solution)/shard_map/all_gather | solution.py:314
  41.3 0.0 copy-done
  41.3 4.6 %build_forward.1 = (bf16[2,128,2048]{2,1,0:T(8,128)(2,1)S(1)}, f32[256,1]{1,0:T(8,128)S(1)}) custom-call(s32[2,128]{1,0:T(2,128)S(1)} %bitcast.23, s32[1]{0:T(128)} %bitcast.1.core_ref, s32[2,40,512]{2,1,0:T(8,128)S(1)} %bitcast.21, s32[1,256]{1,0:T(1,128)S(1)} %bitcast.22), custom_call_target="tpu_custom_call" | custom-call | flops 6000000000 | bytes 6000000 | tf_op jit(solution)/shard_map/build_forward/pallas_call | solution.py:327
  45.9 2.0 %all-to-all-done = bf16[16,4,64,128]{3,2,1,0:T(8,128)(2,1)S(1)} async-done(((bf16[16,4,64,128]{3,2,1,0:T(8,128)(2,1)}), bf16[16,4,64,128]{3,2,1,0:T(8,128)(2,1)S(1)}, u32[]{:S(2)}, u32[]{:S(2)}) %all-to-all-start) | async-done | bytes 1048608 | tf_op jit(solution)/shard_map/all_to_all | solution.py:326
  47.9 0.0 copy-start.1
  47.9 0.0 copy-start.3
  47.9 1.6 %aggregate.1 = (f32[256,128]{1,0:T(8,128)S(1)}, f32[256,128]{1,0:T(8,128)S(1)}) custom-call(s32[2,128]{1,0:T(2,128)S(1)} %bitcast.24, s32[1]{0:T(128)} %bitcast.1.core_ref, bf16[2,128,2048]{2,1,0:T(8,128)(2,1)S(1)} %get-tuple-element.20.tiles_ref, bf16[4096,128]{1,0:T(8,128)(2,1)S(1)} %bitcast.14), custom_call_target="tpu_custom_call" | custom-call | flops 2000000000 | bytes 2000000 | tf_op jit(solution)/shard_map/aggregate/pallas_call | solution.py:336
  49.5 7.4 %all-gather.2 = f32[512,128]{1,0:T(8,128)S(1)} all-gather(f32[256,128]{1,0:T(8,128)S(1)} %get-tuple-element.23), channel_id=4, replica_groups=mesh['zh'=4,'x'=4,'y'=4,'c'=2,'zl'=4] {'c'}, dimensions={0}, use_global_device_ids=true | all-gather | bytes 393216 | tf_op jit(solution)/shard_map/all_gather | solution.py:344
  56.9 0.7 combine.1
  57.6 3.3 %all-to-all-start.1 = ((bf16[4,64,128]{2,1,0:T(8,128)(2,1)}), bf16[4,64,128]{2,1,0:T(8,128)(2,1)S(1)}, u32[]{:S(2)}, u32[]{:S(2)}) async-start(bf16[4,64,128]{2,1,0:T(8,128)(2,1)} %combine.1), calls=%async_computation.1 | async-start | bytes 131072 | tf_op jit(solution)/shard_map/all_to_all | solution.py:347
  60.9 0.1 reshape.20.degree_ref
  61.0 0.1 reshape.22.slot_ref
  61.1 4.5 %all-to-all-done.1.panel_ref = bf16[4,64,128]{2,1,0:T(8,128)(2,1)S(1)} async-done(((bf16[4,64,128]{2,1,0:T(8,128)(2,1)}), bf16[4,64,128]{2,1,0:T(8,128)(2,1)S(1)}, u32[]{:S(2)}, u32[]{:S(2)}) %all-to-all-start.1) | async-done | bytes 65568 | tf_op jit(solution)/shard_map/all_to_all | solution.py:347
  65.6 0.0 copy-done.1
  65.6 0.0 copy-done.3
  65.6 1.4 %dense.1 = (bf16[64,512]{1,0:T(8,128)(2,1)}, bf16[4,64,128]{2,1,0:T(8,128)(2,1)S(1)}, bf16[512,512]{1,0:T(8,128)(2,1)}) custom-call(s32[1]{0:T(128)} %bitcast.part_ref, bf16[4,64,128]{2,1,0:T(8,128)(2,1)S(1)} %all-to-all-done.1.panel_ref, bf16[512,512]{1,0:T(8,128)(2,1)S(1)} %copy-done.1, bf16[64,512]{1,0:T(8,128)(2,1)S(1)} %copy-done.3, ...), custom_call_target="tpu_custom_call" | custom-call | flops 2000000000 | bytes 2000000 | tf_op jit(solution)/shard_map/dense/pallas_call | solution.py:348
  67.0 5.0 %all-to-all-start.2 = ((bf16[32,16,512]{2,1,0:T(8,128)(2,1)}), bf16[32,16,512]{2,1,0:T(8,128)(2,1)S(1)}, u32[]{:S(2)}, u32[]{:S(2)}) async-start(bf16[32,16,512]{2,1,0:T(8,128)(2,1)} %bitcast.9), calls=%async_computation.2 | async-start | bytes 1048576 | tf_op jit(solution)/shard_map/all_to_all | solution.py:355
  72.0 4.4 %build_backward.1.adj_ref = bf16[2048,1024]{1,0:T(8,128)(2,1)S(1)} custom-call(s32[128]{0:T(128)S(1)} %reshape.22.slot_ref, s32[1]{0:T(128)} %bitcast.10.quarter_ref, bf16[4,208,128]{2,1,0:T(8,128)(2,1)S(1)} %bitcast.19), custom_call_target="tpu_custom_call" | custom-call | flops 6000000000 | bytes 6000000 | tf_op jit(solution)/shard_map/build_backward/pallas_call | solution.py:356
  76.5 0.0 copy-start.5
  76.5 2.0 %copy-done.5 = bf16[2048,1024]{1,0:T(8,128)(2,1)} copy-done((bf16[2048,1024]{1,0:T(8,128)(2,1)}, bf16[2048,1024]{1,0:T(8,128)(2,1)S(1)}, u32[]{:S(2)}) %copy-start.5) | copy-done | bytes 4194328
  78.4 5.2 %all-to-all-done.2.part_ref = bf16[32,16,512]{2,1,0:T(8,128)(2,1)S(1)} async-done(((bf16[32,16,512]{2,1,0:T(8,128)(2,1)}), bf16[32,16,512]{2,1,0:T(8,128)(2,1)S(1)}, u32[]{:S(2)}, u32[]{:S(2)}) %all-to-all-start.2) | async-done | bytes 524320 | tf_op jit(solution)/shard_map/all_to_all | solution.py:355
  83.7 0.0 copy-start.6
  83.7 0.1 pack_panels.1
  83.7 8.3 %all_to_all.25.panel_ref = bf16[4,128,128]{2,1,0:T(8,128)(2,1)S(1)} all-to-all(bf16[4,128,128]{2,1,0:T(8,128)(2,1)S(1)} %pack_panels.1), channel_id=1, replica_groups=mesh['zh'=4,'x'=4,'y'=4,'c'=2,'zl'=4] {'zl'}, dimensions={0} | all-to-all | bytes 262144 | tf_op jit(solution)/shard_map/all_to_all | solution.py:366
  92.0 16.5 %all-gather.3 = bf16[1280,128]{1,0:T(8,128)(2,1)S(1)} all-gather(bf16[320,128]{1,0:T(8,128)(2,1)S(1)} %merge_panels.1), channel_id=5, replica_groups=mesh['zh'=4,'x'=4,'y'=4,'c'=2,'zl'=4] {'zh'}, dimensions={0}, use_global_device_ids=true | all-gather | bytes 409600 | tf_op jit(solution)/shard_map/all_gather | solution.py:368
  108.6 0.0 copy-done.6
  108.6 0.0 copy-start.7
  108.6 1.3 spread_back.1
  109.8 25.0 %all_to_all.26.plane_ref = bf16[32,128,128]{2,1,0:T(8,128)(2,1)S(1)} all-to-all(bf16[32,128,128]{2,1,0:T(8,128)(2,1)S(1)} %spread_back.1), channel_id=1, replica_groups=mesh['zh'=4,'x'=4,'y'=4,'c'=2,'zl'=4] {'x','y','c'}, dimensions={0} | all-to-all | bytes 2097152 | tf_op jit(solution)/shard_map/all_to_all | solution.py:376
  134.9 0.0 copy-done.7
  134.9 1.1 finish.1
  (3 shorter events, 0.0 us)
Async XLA Ops:
  1.3 34.3 %copy-start.2 = (s32[1,32,512]{2,1,0:T(8,128)S(1)}, s32[1,32,512]{2,1,0:T(8,128)}, u32[]{:S(2)}) copy-start(s32[1,32,512]{2,1,0:T(8,128)} %edge_hbm.1) | copy-start | bytes 196612
  1.3 34.3 %copy-start.4 = (s32[1,32]{1,0:T(1,128)S(1)}, s32[1,32]{1,0:T(1,128)}, u32[]{:S(2)}) copy-start(s32[1,32]{1,0:T(1,128)} %slot_hbm.1) | copy-start | bytes 388
  27.7 13.5 %copy-start = (s32[256]{0:T(256)S(1)}, s32[256]{0:T(256)}, u32[]{:S(2)}) copy-start(s32[256]{0:T(256)} %param.14) | copy-start | bytes 3076
  28.8 19.1 %all-to-all-start = ((bf16[16,4,64,128]{3,2,1,0:T(8,128)(2,1)}), bf16[16,4,64,128]{3,2,1,0:T(8,128)(2,1)S(1)}, u32[]{:S(2)}, u32[]{:S(2)}) async-start(bf16[16,4,64,128]{3,2,1,0:T(8,128)(2,1)} %fan_out.1), calls=%async_computation | async-start | bytes 2097152 | tf_op jit(solution)/shard_map/all_to_all | solution.py:326
  47.9 17.7 %copy-start.1 = (bf16[512,512]{1,0:T(8,128)(2,1)S(1)}, bf16[512,512]{1,0:T(8,128)(2,1)}, u32[]{:S(2)}) copy-start(bf16[512,512]{1,0:T(8,128)(2,1)} %weight_ref.1) | copy-start | bytes 1572868
  47.9 17.7 %copy-start.3 = (bf16[64,512]{1,0:T(8,128)(2,1)S(1)}, bf16[64,512]{1,0:T(8,128)(2,1)}, u32[]{:S(2)}) copy-start(bf16[64,512]{1,0:T(8,128)(2,1)} %cot_ref.1) | copy-start | bytes 196612
  57.6 8.0 %all-to-all-start.1 = ((bf16[4,64,128]{2,1,0:T(8,128)(2,1)}), bf16[4,64,128]{2,1,0:T(8,128)(2,1)S(1)}, u32[]{:S(2)}, u32[]{:S(2)}) async-start(bf16[4,64,128]{2,1,0:T(8,128)(2,1)} %combine.1), calls=%async_computation.1 | async-start | bytes 131072 | tf_op jit(solution)/shard_map/all_to_all | solution.py:347
  67.0 16.7 %all-to-all-start.2 = ((bf16[32,16,512]{2,1,0:T(8,128)(2,1)}), bf16[32,16,512]{2,1,0:T(8,128)(2,1)S(1)}, u32[]{:S(2)}, u32[]{:S(2)}) async-start(bf16[32,16,512]{2,1,0:T(8,128)(2,1)} %bitcast.9), calls=%async_computation.2 | async-start | bytes 1048576 | tf_op jit(solution)/shard_map/all_to_all | solution.py:355
  76.5 2.0 %copy-start.5 = (bf16[2048,1024]{1,0:T(8,128)(2,1)}, bf16[2048,1024]{1,0:T(8,128)(2,1)S(1)}, u32[]{:S(2)}) copy-start(bf16[2048,1024]{1,0:T(8,128)(2,1)S(1)} %build_backward.1.adj_ref) | copy-start | bytes 12582916
  83.7 24.9 %copy-start.6 = (bf16[2048,1024]{1,0:T(8,128)(2,1)S(1)}, bf16[2048,1024]{1,0:T(8,128)(2,1)}, u32[]{:S(2)}) copy-start(bf16[2048,1024]{1,0:T(8,128)(2,1)} %copy-done.5) | copy-start | bytes 12582916
  108.6 26.3 %copy-start.7 = (f32[64,1]{1,0:T(8,128)S(1)}, f32[64,1]{1,0:T(8,128)}, u32[]{:S(2)}) copy-start(f32[64,1]{1,0:T(8,128)} %get-tuple-element.30.scale_ref) | copy-start | bytes 772

commit v7 on v6

--- a/solution.py
+++ b/solution.py
@@ -268,7 +268,8 @@
         terms = jnp.dot(rows, grad[...], preferred_element_type=jnp.float32).astype(jnp.bfloat16)
         for k in range(4):
             out_ref[i * 4 + k, 0:SUB, :] = terms[k * SUB:(k + 1) * SUB, :]
-            out_ref[i * 4 + k, SUB:TILE, :] = piece
+            half = (k % 2) * 32
+            out_ref[i * 4 + k, SUB:96, :] = piece[half:half + 32, :]
 
 
 def finish(plane_ref, scale_ref, feature_ref, weight_ref):
@@ -277,10 +278,8 @@
         total = total + plane_ref[s, 0:SUB, :].astype(jnp.float32)
     feature_ref[...] = (total * scale_ref[...]).astype(jnp.bfloat16)
     for s in range(32):
-        for p in range(4):
-            weight_ref[s * 16:(s + 1) * 16, p * TILE:(p + 1) * TILE] = plane_ref[
-                s, SUB + p * 16:SUB + (p + 1) * 16, :
-            ].astype(jnp.float32)
+        for p in range(2):
+            weight_ref[s * 16:(s + 1) * 16, p * TILE:(p + 1) * TILE] = plane_ref[s, SUB + p * 16:SUB + (p + 1) * 16, :]
 
 
 def local(features, weight, cotangent, tile_slot, tile_count, tile_edges, deg_dst, deg_src):
@@ -368,15 +367,17 @@
     ring = lax.all_gather(merged, "zh")
     plane = call(
         spread_back,
-        shape((32, TILE, TILE), bf16),
+        shape((32, 96, TILE), bf16),
         [VMEM] * 2,
         [pltpu.VMEM((1024, TILE), bf16)],
         name="spread_back",
     )(adjacent, ring)
     plane = lax.all_to_all(plane, PLANE, 0, 0)
-    feature_grad, weight_grad = call(
-        finish, (shape((SUB, TILE), bf16), shape((512, 512), jnp.float32)), [VMEM] * 2, name="finish"
+    feature_grad, half = call(
+        finish, (shape((SUB, TILE), bf16), shape((512, 256), bf16)), [VMEM] * 2, name="finish"
     )(plane, src_scale)
+    halves = lax.all_gather(half, "c")
+    weight_grad = jnp.concatenate([halves[0], halves[1]], axis=1).astype(jnp.float32)
     return (activated, weight_grad, feature_grad)
 
 

time: 136 us -> 137 us (level)
    all_to_all x1, blocking collectives: 25 us -> 22.4 us  [local(): plane = lax.all_to_all(plane, PLANE, 0, 0)]
    all_gather x0 -> x1, blocking collectives: none -> 2.17 us  [local(): halves = lax.all_gather(half, 'c')]
where the time goes in v7:
time: 137 us; the launch traced here: 136 us
  blocking collectives  87 us (64%)
  Pallas kernels  17.7 us (13%)
  starting transfers between devices  15.1 us (11%)
  waiting for transfers between devices  11.7 us (9%)
  local copies, waits for them, and re-layouts  2.19 us (2%)
  between operations  1.41 us (1%)
    all_gather x1, blocking collectives, local(): ring_piece = lax.all_gather(piece, 'zh')  24.8 us
    all_to_all x1, blocking collectives, local(): plane = lax.all_to_all(plane, PLANE, 0, 0)  22.4 us
    all_gather x1, blocking collectives, local(): ring = lax.all_gather(merged, 'zh')  16.5 us
    all_to_all x1, blocking collectives, local(): panels = lax.all_to_all(panels, 'zl', 0, 0)  8.28 us
    all_gather x1, blocking collectives, local(): lax.all_gather(other_sum, 'c')  7.41 us
    all_to_all x1, starting transfers between devices, local(): plane_sources = lax.all_to_all(copies, ('x', 'y'), 0, 0)  6.77 us
    all_to_all x1, waiting for transfers between devices, local(): parts = lax.all_to_all(terms.reshape(32, 16, 512), PLANE, 0, 0)  5.55 us
    all_gather x1, blocking collectives, local(): codes = lax.all_gather(code, 'c')  5.54 us
  transfers between devices with their start and end apart: 3, of which 3 were waited for; matrix products, arithmetic and copies ran while one was open for 0% of the time, Pallas kernels for 7%

profile of v7, /device:TPU:1, one launch (start us, length us, event | category | flops | bytes accessed | tf_op | source)
XLA Modules:
  0.0 136.2 jit_solution(12688370497550807320)
XLA Ops:
  1.3 0.0 copy-start.2
  1.3 0.0 copy-start.4
  1.3 1.7 %prepare.1 = (bf16[208,128]{1,0:T(8,128)(2,1)}, f32[64,1]{1,0:T(8,128)}) custom-call(s32[1]{0:T(128)S(6)} %copy.14.count_ref, bf16[64,128]{1,0:T(8,128)(2,1)} %feature_hbm.1, s32[1,64]{1,0:T(1,128)} %bitcast.25, s32[1,32]{1,0:T(1,128)} %slot_hbm.1, s32[1,32,512]{2,1,0:T(8,128)} %edge_hbm.1), custom_call_target="tpu_custom_call" | custom-call | flops 1000000000 | bytes 1000000 | tf_op jit(solution)/shard_map/prepare/pallas_call | solution.py:290
  3.0 24.8 %all-gather.1 = bf16[832,128]{1,0:T(8,128)(2,1)S(1)} all-gather(bf16[208,128]{1,0:T(8,128)(2,1)} %get-tuple-element.18), channel_id=3, replica_groups=mesh['zh'=4,'x'=4,'y'=4,'c'=2,'zl'=4] {'zh'}, dimensions={0}, use_global_device_ids=true | all-gather | bytes 266240 | tf_op jit(solution)/shard_map/all_gather | solution.py:312
  27.7 0.0 copy-start
  27.7 1.1 fan_out.1
  28.8 6.8 %all-to-all-start = ((bf16[16,4,64,128]{3,2,1,0:T(8,128)(2,1)}), bf16[16,4,64,128]{3,2,1,0:T(8,128)(2,1)S(1)}, u32[]{:S(2)}, u32[]{:S(2)}) async-start(bf16[16,4,64,128]{3,2,1,0:T(8,128)(2,1)} %fan_out.1), calls=%async_computation | async-start | bytes 2097152 | tf_op jit(solution)/shard_map/all_to_all | solution.py:325
  35.6 0.0 copy-done.2
  35.6 0.0 copy-done.4
  35.6 0.1 mark_edges.1
  35.7 5.5 %all-gather = s32[80,512]{1,0:T(8,128)S(1)} all-gather(s32[40,512]{1,0:T(8,128)S(1)} %mark_edges.1), channel_id=2, replica_groups=mesh['zh'=4,'x'=4,'y'=4,'c'=2,'zl'=4] {'c'}, dimensions={0}, use_global_device_ids=true | all-gather | bytes 245760 | tf_op jit(solution)/shard_map/all_gather | solution.py:313
  41.3 0.0 copy-done
  41.3 5.0 %build_forward.1 = (bf16[2,128,2048]{2,1,0:T(8,128)(2,1)S(1)}, f32[256,1]{1,0:T(8,128)S(1)}) custom-call(s32[2,128]{1,0:T(2,128)S(1)} %bitcast.23, s32[1]{0:T(128)} %bitcast.1.core_ref, s32[2,40,512]{2,1,0:T(8,128)S(1)} %bitcast.21, s32[1,256]{1,0:T(1,128)S(1)} %bitcast.22), custom_call_target="tpu_custom_call" | custom-call | flops 6000000000 | bytes 6000000 | tf_op jit(solution)/shard_map/build_forward/pallas_call | solution.py:326
  46.3 1.6 %all-to-all-done = bf16[16,4,64,128]{3,2,1,0:T(8,128)(2,1)S(1)} async-done(((bf16[16,4,64,128]{3,2,1,0:T(8,128)(2,1)}), bf16[16,4,64,128]{3,2,1,0:T(8,128)(2,1)S(1)}, u32[]{:S(2)}, u32[]{:S(2)}) %all-to-all-start) | async-done | bytes 1048608 | tf_op jit(solution)/shard_map/all_to_all | solution.py:325
  47.9 0.0 copy-start.1
  47.9 0.0 copy-start.3
  47.9 1.6 %aggregate.1 = (f32[256,128]{1,0:T(8,128)S(1)}, f32[256,128]{1,0:T(8,128)S(1)}) custom-call(s32[2,128]{1,0:T(2,128)S(1)} %bitcast.24, s32[1]{0:T(128)} %bitcast.1.core_ref, bf16[2,128,2048]{2,1,0:T(8,128)(2,1)S(1)} %get-tuple-element.20.tiles_ref, bf16[4096,128]{1,0:T(8,128)(2,1)S(1)} %bitcast.14), custom_call_target="tpu_custom_call" | custom-call | flops 2000000000 | bytes 2000000 | tf_op jit(solution)/shard_map/aggregate/pallas_call | solution.py:335
  49.5 7.4 %all-gather.2 = f32[512,128]{1,0:T(8,128)S(1)} all-gather(f32[256,128]{1,0:T(8,128)S(1)} %get-tuple-element.23), channel_id=4, replica_groups=mesh['zh'=4,'x'=4,'y'=4,'c'=2,'zl'=4] {'c'}, dimensions={0}, use_global_device_ids=true | all-gather | bytes 393216 | tf_op jit(solution)/shard_map/all_gather | solution.py:343
  56.9 0.7 combine.1
  57.6 3.3 %all-to-all-start.1 = ((bf16[4,64,128]{2,1,0:T(8,128)(2,1)}), bf16[4,64,128]{2,1,0:T(8,128)(2,1)S(1)}, u32[]{:S(2)}, u32[]{:S(2)}) async-start(bf16[4,64,128]{2,1,0:T(8,128)(2,1)} %combine.1), calls=%async_computation.1 | async-start | bytes 131072 | tf_op jit(solution)/shard_map/all_to_all | solution.py:346
  60.9 0.1 reshape.20.degree_ref
  61.0 0.1 reshape.22.slot_ref
  61.1 4.5 %all-to-all-done.1.panel_ref = bf16[4,64,128]{2,1,0:T(8,128)(2,1)S(1)} async-done(((bf16[4,64,128]{2,1,0:T(8,128)(2,1)}), bf16[4,64,128]{2,1,0:T(8,128)(2,1)S(1)}, u32[]{:S(2)}, u32[]{:S(2)}) %all-to-all-start.1) | async-done | bytes 65568 | tf_op jit(solution)/shard_map/all_to_all | solution.py:346
  65.6 0.0 copy-done.1
  65.6 0.0 copy-done.3
  65.6 1.4 %dense.1 = (bf16[64,512]{1,0:T(8,128)(2,1)}, bf16[4,64,128]{2,1,0:T(8,128)(2,1)S(1)}, bf16[512,512]{1,0:T(8,128)(2,1)}) custom-call(s32[1]{0:T(128)} %bitcast.part_ref, bf16[4,64,128]{2,1,0:T(8,128)(2,1)S(1)} %all-to-all-done.1.panel_ref, bf16[512,512]{1,0:T(8,128)(2,1)S(1)} %copy-done.1, bf16[64,512]{1,0:T(8,128)(2,1)S(1)} %copy-done.3, ...), custom_call_target="tpu_custom_call" | custom-call | flops 2000000000 | bytes 2000000 | tf_op jit(solution)/shard_map/dense/pallas_call | solution.py:347
  67.0 5.0 %all-to-all-start.2 = ((bf16[32,16,512]{2,1,0:T(8,128)(2,1)}), bf16[32,16,512]{2,1,0:T(8,128)(2,1)S(1)}, u32[]{:S(2)}, u32[]{:S(2)}) async-start(bf16[32,16,512]{2,1,0:T(8,128)(2,1)} %bitcast.9), calls=%async_computation.2 | async-start | bytes 1048576 | tf_op jit(solution)/shard_map/all_to_all | solution.py:354
  72.0 4.1 %build_backward.1.adj_ref = bf16[2048,1024]{1,0:T(8,128)(2,1)S(1)} custom-call(s32[128]{0:T(128)S(1)} %reshape.22.slot_ref, s32[1]{0:T(128)} %bitcast.10.quarter_ref, bf16[4,208,128]{2,1,0:T(8,128)(2,1)S(1)} %bitcast.19), custom_call_target="tpu_custom_call" | custom-call | flops 6000000000 | bytes 6000000 | tf_op jit(solution)/shard_map/build_backward/pallas_call | solution.py:355
  76.1 0.0 copy-start.5
  76.1 2.0 %copy-done.5 = bf16[2048,1024]{1,0:T(8,128)(2,1)} copy-done((bf16[2048,1024]{1,0:T(8,128)(2,1)}, bf16[2048,1024]{1,0:T(8,128)(2,1)S(1)}, u32[]{:S(2)}) %copy-start.5) | copy-done | bytes 4194328
  78.1 5.6 %all-to-all-done.2.part_ref = bf16[32,16,512]{2,1,0:T(8,128)(2,1)S(1)} async-done(((bf16[32,16,512]{2,1,0:T(8,128)(2,1)}), bf16[32,16,512]{2,1,0:T(8,128)(2,1)S(1)}, u32[]{:S(2)}, u32[]{:S(2)}) %all-to-all-start.2) | async-done | bytes 524320 | tf_op jit(solution)/shard_map/all_to_all | solution.py:354
  83.7 0.0 copy-start.6
  83.7 0.1 pack_panels.1
  83.7 8.3 %all_to_all.25.panel_ref = bf16[4,128,128]{2,1,0:T(8,128)(2,1)S(1)} all-to-all(bf16[4,128,128]{2,1,0:T(8,128)(2,1)S(1)} %pack_panels.1), channel_id=1, replica_groups=mesh['zh'=4,'x'=4,'y'=4,'c'=2,'zl'=4] {'zl'}, dimensions={0} | all-to-all | bytes 262144 | tf_op jit(solution)/shard_map/all_to_all | solution.py:365
  92.0 16.5 %all-gather.3 = bf16[1280,128]{1,0:T(8,128)(2,1)S(1)} all-gather(bf16[320,128]{1,0:T(8,128)(2,1)S(1)} %merge_panels.1), channel_id=5, replica_groups=mesh['zh'=4,'x'=4,'y'=4,'c'=2,'zl'=4] {'zh'}, dimensions={0}, use_global_device_ids=true | all-gather | bytes 409600 | tf_op jit(solution)/shard_map/all_gather | solution.py:367
  108.6 0.0 copy-done.6
  108.6 0.0 copy-start.7
  108.6 1.3 spread_back.1
  109.8 22.4 %all_to_all.26.plane_ref = bf16[32,96,128]{2,1,0:T(8,128)(2,1)S(1)} all-to-all(bf16[32,96,128]{2,1,0:T(8,128)(2,1)S(1)} %spread_back.1), channel_id=1, replica_groups=mesh['zh'=4,'x'=4,'y'=4,'c'=2,'zl'=4] {'x','y','c'}, dimensions={0} | all-to-all | bytes 1572864 | tf_op jit(solution)/shard_map/all_to_all | solution.py:375
  132.2 0.0 copy-done.7
  132.2 0.7 finish.1
  132.9 2.2 %all-gather.4 = bf16[1024,256]{1,0:T(8,128)(2,1)S(1)} all-gather(bf16[512,256]{1,0:T(8,128)(2,1)S(1)} %get-tuple-element.31), channel_id=6, replica_groups=mesh['zh'=4,'x'=4,'y'=4,'c'=2,'zl'=4] {'c'}, dimensions={0}, use_global_device_ids=true | all-gather | bytes 786432 | tf_op jit(solution)/shard_map/all_gather | solution.py:379
  135.1 1.1 maximum_convert_fusion
  (4 shorter events, 0.1 us)
Async XLA Ops:
  1.3 34.3 %copy-start.2 = (s32[1,32,512]{2,1,0:T(8,128)S(1)}, s32[1,32,512]{2,1,0:T(8,128)}, u32[]{:S(2)}) copy-start(s32[1,32,512]{2,1,0:T(8,128)} %edge_hbm.1) | copy-start | bytes 196612
  1.3 34.3 %copy-start.4 = (s32[1,32]{1,0:T(1,128)S(1)}, s32[1,32]{1,0:T(1,128)}, u32[]{:S(2)}) copy-start(s32[1,32]{1,0:T(1,128)} %slot_hbm.1) | copy-start | bytes 388
  27.7 13.5 %copy-start = (s32[256]{0:T(256)S(1)}, s32[256]{0:T(256)}, u32[]{:S(2)}) copy-start(s32[256]{0:T(256)} %param.14) | copy-start | bytes 3076
  28.8 19.1 %all-to-all-start = ((bf16[16,4,64,128]{3,2,1,0:T(8,128)(2,1)}), bf16[16,4,64,128]{3,2,1,0:T(8,128)(2,1)S(1)}, u32[]{:S(2)}, u32[]{:S(2)}) async-start(bf16[16,4,64,128]{3,2,1,0:T(8,128)(2,1)} %fan_out.1), calls=%async_computation | async-start | bytes 2097152 | tf_op jit(solution)/shard_map/all_to_all | solution.py:325
  47.9 17.7 %copy-start.1 = (bf16[512,512]{1,0:T(8,128)(2,1)S(1)}, bf16[512,512]{1,0:T(8,128)(2,1)}, u32[]{:S(2)}) copy-start(bf16[512,512]{1,0:T(8,128)(2,1)} %weight_ref.1) | copy-start | bytes 1572868
  47.9 17.7 %copy-start.3 = (bf16[64,512]{1,0:T(8,128)(2,1)S(1)}, bf16[64,512]{1,0:T(8,128)(2,1)}, u32[]{:S(2)}) copy-start(bf16[64,512]{1,0:T(8,128)(2,1)} %cot_ref.1) | copy-start | bytes 196612
  57.6 8.0 %all-to-all-start.1 = ((bf16[4,64,128]{2,1,0:T(8,128)(2,1)}), bf16[4,64,128]{2,1,0:T(8,128)(2,1)S(1)}, u32[]{:S(2)}, u32[]{:S(2)}) async-start(bf16[4,64,128]{2,1,0:T(8,128)(2,1)} %combine.1), calls=%async_computation.1 | async-start | bytes 131072 | tf_op jit(solution)/shard_map/all_to_all | solution.py:346
  67.0 16.7 %all-to-all-start.2 = ((bf16[32,16,512]{2,1,0:T(8,128)(2,1)}), bf16[32,16,512]{2,1,0:T(8,128)(2,1)S(1)}, u32[]{:S(2)}, u32[]{:S(2)}) async-start(bf16[32,16,512]{2,1,0:T(8,128)(2,1)} %bitcast.9), calls=%async_computation.2 | async-start | bytes 1048576 | tf_op jit(solution)/shard_map/all_to_all | solution.py:354
  76.1 2.0 %copy-start.5 = (bf16[2048,1024]{1,0:T(8,128)(2,1)}, bf16[2048,1024]{1,0:T(8,128)(2,1)S(1)}, u32[]{:S(2)}) copy-start(bf16[2048,1024]{1,0:T(8,128)(2,1)S(1)} %build_backward.1.adj_ref) | copy-start | bytes 12582916
  83.7 24.9 %copy-start.6 = (bf16[2048,1024]{1,0:T(8,128)(2,1)S(1)}, bf16[2048,1024]{1,0:T(8,128)(2,1)}, u32[]{:S(2)}) copy-start(bf16[2048,1024]{1,0:T(8,128)(2,1)} %copy-done.5) | copy-start | bytes 12582916
  108.6 23.6 %copy-start.7 = (f32[64,1]{1,0:T(8,128)S(1)}, f32[64,1]{1,0:T(8,128)}, u32[]{:S(2)}) copy-start(f32[64,1]{1,0:T(8,128)} %get-tuple-element.30.scale_ref) | copy-start | bytes 772
